TPU v7x, 32 devices: a whole 2x2x4 slice. The times are simulated.
32 devices in a mesh: seq: 8 (over z, x), head: 4 (over y, core).
Axes of the slice: x: 2, y: 2, z: 4, core: 2. Of those that a mesh axis runs over, the one named last changes fastest.
Arguments:
- queries: bfloat16 [8192, 32, 128], P('seq', 'head'), may hold values from -6 to 6
- seg_keys: bfloat16 [8192, 32, 128], P('seq', 'head'), may hold values from -6 to 6
- seg_values: bfloat16 [8192, 32, 128], P('seq', 'head'), may hold values from -6 to 6
- mem_keys: bfloat16 [32768, 32, 128], P('seq', 'head'), may hold values from -6 to 6
- mem_values: bfloat16 [32768, 32, 128], P('seq', 'head'), may hold values from -6 to 6
- mem_blocks: int32 [64, 4], P(('seq', 'head')), may hold values from 0 to 255, as said below
- mem_count: int32 [64], P(('seq', 'head')), may hold values from 1 to 4, as said below
- grad_out: bfloat16 [8192, 32, 128], P('seq', 'head'), may hold values from -6 to 6
Outputs:
- attn_out: bfloat16 [8192, 32, 128], P('seq', 'head')
- grad_q: bfloat16 [8192, 32, 128], P('seq', 'head')
- grad_k: bfloat16 [8192, 32, 128], P('seq', 'head')
- grad_v: bfloat16 [8192, 32, 128], P('seq', 'head')
Inputs may be any that keep to these rules, and one draw needn't show every extreme that they name: `mem_blocks`: block n is held by owner n // 32. Among the 32 entries of the 8 query blocks of one seq shard (aligned blocks of 8 rows), at most 8 lie with one owner, and one owner has exactly 8 from every shard. Among the used entries (s < mem_count) of one seq shard at most 5 lie with one owner, and that same owner has exactly 5 used entries from every shard. `mem_count`: the counts of the 8 query blocks of one seq shard (aligned blocks of 8 rows) add up to 20, and in every such block of rows one count is 4.
All inputs are finite; a program needn't handle non-finite values.
Results may differ from a plain program's by a relative error of at most 0.012.
Values may be sent and summed in bfloat16 or wider, within the bound.
No kernel may reach another device: no remote copies, remote signals or barrier semaphores. Data moves between devices by JAX's collectives and lax.ppermute only.
A program may use at most 192 MiB of HBM per device.

v0:
```python
import math

import jax
import jax.numpy as jnp
from jax import lax
from jax.sharding import PartitionSpec as P

WINDOW = 1024
BLOCK = 128
TOPK = 4


def passed_along(block, axis, distance):
    devices = range(lax.axis_size(axis))
    route = [(i - distance, i) for i in devices if i - distance in devices]
    return lax.ppermute(block, axis, route)


def fetch_memory(block_lists, block_counts, mem_keys, mem_values, owners, live_capacity):
    n_rows, top_count = block_lists.shape
    mem_local = mem_keys.shape[0] // BLOCK
    head_count = mem_keys.shape[1]
    head_dim = mem_keys.shape[2]
    flat_ids = block_lists.reshape(-1)
    owner_of = flat_ids // mem_local
    inside_id = flat_ids % mem_local
    one_hot = (owner_of[:, None] == jnp.arange(owners, dtype=jnp.int32)[None, :]).astype(jnp.int32)
    key_blocks = mem_keys.reshape(mem_local, BLOCK, head_count, head_dim)
    value_blocks = mem_values.reshape(mem_local, BLOCK, head_count, head_dim)
    live_flag = (jnp.arange(top_count, dtype=jnp.int32)[None, :] < block_counts[:, None]).reshape(
        -1
    )
    live_hot = one_hot * live_flag.astype(jnp.int32)[:, None]
    order_in = jnp.sum((jnp.cumsum(live_hot, 0) - 1) * live_hot, 1)
    slot_of = jnp.where(live_flag, owner_of * live_capacity + order_in, owners * live_capacity)
    send_table = (
        jnp.zeros((owners * live_capacity,), jnp.int32)
        .at[slot_of]
        .set(inside_id, mode="drop")
        .reshape(owners, live_capacity)
    )
    wanted = lax.all_to_all(send_table, "seq", split_axis=0, concat_axis=0, tiled=True)
    got_keys = lax.all_to_all(
        jnp.take(key_blocks, wanted, axis=0), "seq", split_axis=0, concat_axis=0, tiled=True
    )
    got_values = lax.all_to_all(
        jnp.take(value_blocks, wanted, axis=0), "seq", split_axis=0, concat_axis=0, tiled=True
    )
    read_slot = jnp.where(live_flag, slot_of, 0)
    got_keys = got_keys.reshape(owners * live_capacity, BLOCK, head_count, head_dim)[read_slot]
    got_values = got_values.reshape(owners * live_capacity, BLOCK, head_count, head_dim)[read_slot]
    got_keys = got_keys.reshape(n_rows, top_count * BLOCK, head_count, head_dim)
    got_values = got_values.reshape(n_rows, top_count * BLOCK, head_count, head_dim)
    return (jnp.moveaxis(got_keys, 2, 0), jnp.moveaxis(got_values, 2, 0))


def shards(queries, seg_keys, seg_values, mem_keys, mem_values, mem_blocks, mem_count, grad_out):
    local_tokens, head_count, head_dim = queries.shape
    owners = lax.axis_size("seq")
    seq_rank = lax.axis_index("seq")
    n_blocks = local_tokens // BLOCK
    n_tiles = local_tokens // WINDOW
    mem_span = TOPK * BLOCK
    live_total = n_blocks * (TOPK + 1) // 2
    live_capacity = max(2, 2 * live_total // owners)
    score_scale = 1.0 / math.sqrt(head_dim)
    block_lists, block_counts = (
        lax.all_gather(mem_blocks, "head", axis=0, tiled=True),
        lax.all_gather(mem_count, "head", axis=0, tiled=True),
    )
    prev_keys, prev_values = passed_along((seg_keys, seg_values), "seq", 1)
    keys_major = jnp.moveaxis(jnp.concatenate([prev_keys, seg_keys], 0), 1, 0)
    values_major = jnp.moveaxis(jnp.concatenate([prev_values, seg_values], 0), 1, 0)
    queries_major = jnp.moveaxis(queries, 1, 0)
    grads_major = jnp.moveaxis(grad_out, 1, 0)
    row_in = jnp.arange(WINDOW, dtype=jnp.int32)[:, None]
    col_in = jnp.arange(WINDOW, dtype=jnp.int32)[None, :]
    key_glob = (
        seq_rank * local_tokens
        + jnp.arange(n_tiles, dtype=jnp.int32)[:, None, None] * WINDOW
        + col_in[None]
        - WINDOW
    )
    lower_mask = (col_in > row_in)[None] & (key_glob >= 0)
    upper_mask = col_in <= row_in
    mem_slot = jnp.arange(mem_span, dtype=jnp.int32) // BLOCK
    far_mask = mem_slot[None, None, :] < block_counts[:, None, None]
    mem_k, mem_v = fetch_memory(
        block_lists, block_counts, mem_keys, mem_values, owners, live_capacity
    )

    def score_parts(query_rows, key_rows, mem_key_rows):
        query_tiles = query_rows.reshape(n_tiles, WINDOW, head_dim)
        key_tiles = key_rows.reshape(n_tiles + 1, WINDOW, head_dim)
        lower = (
            jnp.einsum(
                "twd,tjd->twj", query_tiles, key_tiles[:-1], preferred_element_type=jnp.float32
            )
            * score_scale
        )
        upper = (
            jnp.einsum(
                "twd,tjd->twj", query_tiles, key_tiles[1:], preferred_element_type=jnp.float32
            )
            * score_scale
        )
        far = (
            jnp.einsum(
                "nbd,nmd->nbm",
                query_rows.reshape(n_blocks, BLOCK, head_dim),
                mem_key_rows,
                preferred_element_type=jnp.float32,
            )
            * score_scale
        )
        lower = jnp.where(lower_mask, lower, -jnp.inf)
        upper = jnp.where(upper_mask[None], upper, -jnp.inf)
        far = jnp.where(far_mask, far, -jnp.inf)
        return (lower, upper, far)

    def probabilities(lower, upper, far, lse_tiles):
        lower_p = jnp.exp(lower - lse_tiles[:, :, None])
        upper_p = jnp.exp(upper - lse_tiles[:, :, None])
        far_p = jnp.exp(far - lse_tiles.reshape(n_blocks, BLOCK)[:, :, None])
        return (lower_p, upper_p, far_p)

    def mix(lower_w, upper_w, far_w, key_rows, mem_rows):
        key_tiles = key_rows.reshape(n_tiles + 1, WINDOW, head_dim)
        total = jnp.einsum(
            "twj,tjd->twd", lower_w, key_tiles[:-1], preferred_element_type=jnp.float32
        )
        total = total + jnp.einsum(
            "twj,tjd->twd", upper_w, key_tiles[1:], preferred_element_type=jnp.float32
        )
        far_total = jnp.einsum("nbm,nmd->nbd", far_w, mem_rows, preferred_element_type=jnp.float32)
        return total.reshape(local_tokens, head_dim) + far_total.reshape(local_tokens, head_dim)

    def forward_head(packed):
        query_rows, key_rows, value_rows, mem_key_rows, mem_value_rows = packed
        lower, upper, far = score_parts(query_rows, key_rows, mem_key_rows)
        row_top = jnp.maximum(
            jnp.maximum(jnp.max(lower, 2), jnp.max(upper, 2)),
            jnp.max(far, 2).reshape(n_tiles, WINDOW),
        )
        row_sum = jnp.sum(jnp.exp(lower - row_top[:, :, None]), 2) + jnp.sum(
            jnp.exp(upper - row_top[:, :, None]), 2
        )
        row_sum = row_sum + jnp.sum(
            jnp.exp(far - row_top.reshape(n_blocks, BLOCK)[:, :, None]), 2
        ).reshape(n_tiles, WINDOW)
        lse_tiles = row_top + jnp.log(row_sum)
        lower_p, upper_p, far_p = probabilities(lower, upper, far, lse_tiles)
        attn_rows = mix(
            lower_p.astype(jnp.bfloat16),
            upper_p.astype(jnp.bfloat16),
            far_p.astype(jnp.bfloat16),
            value_rows,
            mem_value_rows,
        ).astype(jnp.bfloat16)
        return (attn_rows, lse_tiles.reshape(local_tokens))

    attn_heads, lse_heads = lax.map(
        forward_head, (queries_major, keys_major, values_major, mem_k, mem_v)
    )
    back_k, back_v = (mem_k, mem_v)

    def backward_head(packed):
        (
            query_rows,
            grad_rows,
            key_rows,
            value_rows,
            mem_key_rows,
            mem_value_rows,
            attn_rows,
            lse_rows,
        ) = packed
        lower, upper, far = score_parts(query_rows, key_rows, mem_key_rows)
        lse_tiles = lse_rows.reshape(n_tiles, WINDOW)
        lower_p, upper_p, far_p = probabilities(lower, upper, far, lse_tiles)
        delta_rows = jnp.sum(grad_rows.astype(jnp.float32) * attn_rows.astype(jnp.float32), 1)
        delta_tiles = delta_rows.reshape(n_tiles, WINDOW)
        grad_tiles = grad_rows.reshape(n_tiles, WINDOW, head_dim)
        query_tiles = query_rows.reshape(n_tiles, WINDOW, head_dim)
        value_tiles = value_rows.reshape(n_tiles + 1, WINDOW, head_dim)
        grad_blocks = grad_rows.reshape(n_blocks, BLOCK, head_dim)
        lower_dp = jnp.einsum(
            "twd,tjd->twj", grad_tiles, value_tiles[:-1], preferred_element_type=jnp.float32
        )
        upper_dp = jnp.einsum(
            "twd,tjd->twj", grad_tiles, value_tiles[1:], preferred_element_type=jnp.float32
        )
        far_dp = jnp.einsum(
            "nbd,nmd->nbm", grad_blocks, mem_value_rows, preferred_element_type=jnp.float32
        )
        lower_ds = (lower_p * (lower_dp - delta_tiles[:, :, None])).astype(jnp.bfloat16)
        upper_ds = (upper_p * (upper_dp - delta_tiles[:, :, None])).astype(jnp.bfloat16)
        far_ds = (far_p * (far_dp - delta_rows.reshape(n_blocks, BLOCK)[:, :, None])).astype(
            jnp.bfloat16
        )
        grad_query = (score_scale * mix(lower_ds, upper_ds, far_ds, key_rows, mem_key_rows)).astype(
            jnp.bfloat16
        )
        zero_tile = jnp.zeros((1, WINDOW, head_dim), jnp.float32)
        lower_kg = jnp.einsum(
            "twj,twd->tjd", lower_ds, query_tiles, preferred_element_type=jnp.float32
        )
        upper_kg = jnp.einsum(
            "twj,twd->tjd", upper_ds, query_tiles, preferred_element_type=jnp.float32
        )
        key_grad = score_scale * (
            jnp.concatenate([lower_kg, zero_tile], 0) + jnp.concatenate([zero_tile, upper_kg], 0)
        )
        lower_vg = jnp.einsum(
            "twj,twd->tjd",
            lower_p.astype(jnp.bfloat16),
            grad_tiles,
            preferred_element_type=jnp.float32,
        )
        upper_vg = jnp.einsum(
            "twj,twd->tjd",
            upper_p.astype(jnp.bfloat16),
            grad_tiles,
            preferred_element_type=jnp.float32,
        )
        value_grad = jnp.concatenate([lower_vg, zero_tile], 0) + jnp.concatenate(
            [zero_tile, upper_vg], 0
        )
        ext_rows = (n_tiles + 1) * WINDOW
        return (
            grad_query,
            key_grad.reshape(ext_rows, head_dim),
            value_grad.reshape(ext_rows, head_dim),
            delta_rows,
        )

    gradq_heads, key_ext, value_ext, delta_heads = lax.map(
        backward_head,
        (
            queries_major,
            grads_major,
            keys_major,
            values_major,
            back_k,
            back_v,
            attn_heads,
            lse_heads,
        ),
    )
    own_keys = key_ext[:, WINDOW:]
    own_values = value_ext[:, WINDOW:]
    back_keys, back_values = passed_along((key_ext[:, :WINDOW], value_ext[:, :WINDOW]), "seq", -1)
    own_keys = own_keys + back_keys
    own_values = own_values + back_values
    attn_out = jnp.moveaxis(attn_heads, 0, 1)
    grad_q = jnp.moveaxis(gradq_heads, 0, 1)
    grad_k = jnp.moveaxis(own_keys.astype(jnp.bfloat16), 0, 1)
    grad_v = jnp.moveaxis(own_values.astype(jnp.bfloat16), 0, 1)
    return (attn_out, grad_q, grad_k, grad_v)


def solution(mesh):
    return jax.shard_map(
        shards,
        mesh=mesh,
        in_specs=(
            P("seq", "head", None),
            P("seq", "head", None),
            P("seq", "head", None),
            P("seq", "head", None),
            P("seq", "head", None),
            P(("seq", "head"), None),
            P(("seq", "head")),
            P("seq", "head", None),
        ),
        out_specs=(
            P("seq", "head", None),
            P("seq", "head", None),
            P("seq", "head", None),
            P("seq", "head", None),
        ),
        check_vma=False,
    )
```

profile of v0, /device:TPU:16, one launch (start us, length us, event | category | flops | bytes accessed | tf_op | source)
XLA Modules:
  0.0 1655.1 jit_solution(1082943139767376819)
XLA Ops:
  55.9 230.5 %all_to_all.23 = bf16[8,5,128,8,128]{4,3,2,1,0:T(8,128)(2,1)} all-to-all(bf16[8,5,128,8,128]{4,3,2,1,0:T(8,128)(2,1)S(1)} %get-tuple-element.281), channel_id=1, replica_groups=mesh['seq'=8,'head'=4] {'seq'}, dimensions={0} | all-to-all | bytes 20971520 | tf_op jit(solution)/shard_map/all_to_all | solution.py:46
  307.5 256.7 %collective-permute-done = bf16[1024,8,128]{2,0,1:T(8,128)(2,1)} collective-permute-done((bf16[1024,8,128]{2,0,1:T(8,128)(2,1)}, bf16[1024,8,128]{2,0,1:T(8,128)(2,1)}, u32[]{:S(2)}, u32[]{:S(2)}) %collective-permute-start) | collective-permute-done | bytes 2097184 | tf_op jit(solution)/shard_map/ppermute | solution.py:16
  568.7 40.3 %collective-permute-done.1 = bf16[1024,8,128]{2,0,1:T(8,128)(2,1)} collective-permute-done((bf16[1024,8,128]{2,0,1:T(8,128)(2,1)S(1)}, bf16[1024,8,128]{2,0,1:T(8,128)(2,1)}, u32[]{:S(2)}, u32[]{:S(2)}) %collective-permute-start.1) | collective-permute-done | bytes 2097184 | tf_op jit(solution)/shard_map/ppermute | solution.py:16
  630.8 12.8 copy_bitcast_fusion
  645.3 151.8 %while.28 = (s32[]{:T(128)}, bf16[8,1024,128]{2,1,0:T(8,128)(2,1)}, f32[8,1024]{1,0:T(8,128)S(1)}, bf16[8,1024,128]{2,1,0:T(8,128)(2,1)}, bf16[8,2048,128]{2,1,0...) while((s32[]{:T(128)}, bf16[8,1024,128]{2,1,0:T(8,128)(2,1)}, ...), condition=%wide.region_10.12_spmd.clone, body=%wide.region_3.11_spmd.clone.sunk | while | flops 1378756608 | bytes 55218924 | solution.py:162
  798.7 667.8 %while.29 = (s32[]{:T(128)}, bf16[8,1024,128]{2,1,0:T(8,128)(2,1)}, f32[8,2048,128]{2,0,1:T(8,128)}, f32[8,2048,128]{2,0,1:T(8,128)}, bf16[8,1024,128]{2,1,0:T(8...) while((s32[]{:T(128)}, bf16[8,1024,128]{2,1,0:T(8,128)(2,1)}, ...), condition=%wide.region_13.15_spmd.clone, body=%wide.region_11.14_spmd.clone.sunk | while | flops 3119254528 | bytes 116976568 | solution.py:237
  820.8 28.4 %dynamic_update_slice.33 = f32[8,2048,128]{2,0,1:T(8,128)} dynamic-update-slice(f32[8,2048,128]{2,0,1:T(8,128)} %get-tuple-element.539, f32[1,2048,128]{2,0,1:T(1,128)S(1)} %bitcast.348, s32[]{:T(128)S(6)} %copy.84, s32[]{:T(128)} %constant.120.clone.1..sunk.1, s32[]{:T(128)} %constant.120.clone.1..sunk.1) | dynamic-update-slice | bytes 2097156 | tf_op jit(solution)/shard_map/while/body/jit(dynamic_update_index_in_dim)/dynamic_update_slice | solution.py:237
  853.8 28.4 %dynamic_update_slice.34 = f32[8,2048,128]{2,0,1:T(8,128)} dynamic-update-slice(f32[8,2048,128]{2,0,1:T(8,128)} %get-tuple-element.540, f32[1,2048,128]{2,0,1:T(1,128)S(1)} %bitcast.347, s32[]{:T(128)S(6)} %copy.84, s32[]{:T(128)} %constant.120.clone.1..sunk.1, s32[]{:T(128)} %constant.120.clone.1..sunk.1) | dynamic-update-slice | bytes 2097156 | tf_op jit(solution)/shard_map/while/body/jit(dynamic_update_index_in_dim)/dynamic_update_slice | solution.py:237
  904.3 28.4 %dynamic_update_slice.33 = f32[8,2048,128]{2,0,1:T(8,128)} dynamic-update-slice(f32[8,2048,128]{2,0,1:T(8,128)} %get-tuple-element.539, f32[1,2048,128]{2,0,1:T(1,128)S(1)} %bitcast.348, s32[]{:T(128)S(6)} %copy.84, s32[]{:T(128)} %constant.120.clone.1..sunk.1, s32[]{:T(128)} %constant.120.clone.1..sunk.1) | dynamic-update-slice | bytes 2097156 | tf_op jit(solution)/shard_map/while/body/jit(dynamic_update_index_in_dim)/dynamic_update_slice | solution.py:237
  937.3 28.4 %dynamic_update_slice.34 = f32[8,2048,128]{2,0,1:T(8,128)} dynamic-update-slice(f32[8,2048,128]{2,0,1:T(8,128)} %get-tuple-element.540, f32[1,2048,128]{2,0,1:T(1,128)S(1)} %bitcast.347, s32[]{:T(128)S(6)} %copy.84, s32[]{:T(128)} %constant.120.clone.1..sunk.1, s32[]{:T(128)} %constant.120.clone.1..sunk.1) | dynamic-update-slice | bytes 2097156 | tf_op jit(solution)/shard_map/while/body/jit(dynamic_update_index_in_dim)/dynamic_update_slice | solution.py:237
  987.8 28.4 %dynamic_update_slice.33 = f32[8,2048,128]{2,0,1:T(8,128)} dynamic-update-slice(f32[8,2048,128]{2,0,1:T(8,128)} %get-tuple-element.539, f32[1,2048,128]{2,0,1:T(1,128)S(1)} %bitcast.348, s32[]{:T(128)S(6)} %copy.84, s32[]{:T(128)} %constant.120.clone.1..sunk.1, s32[]{:T(128)} %constant.120.clone.1..sunk.1) | dynamic-update-slice | bytes 2097156 | tf_op jit(solution)/shard_map/while/body/jit(dynamic_update_index_in_dim)/dynamic_update_slice | solution.py:237
  1020.8 28.4 %dynamic_update_slice.34 = f32[8,2048,128]{2,0,1:T(8,128)} dynamic-update-slice(f32[8,2048,128]{2,0,1:T(8,128)} %get-tuple-element.540, f32[1,2048,128]{2,0,1:T(1,128)S(1)} %bitcast.347, s32[]{:T(128)S(6)} %copy.84, s32[]{:T(128)} %constant.120.clone.1..sunk.1, s32[]{:T(128)} %constant.120.clone.1..sunk.1) | dynamic-update-slice | bytes 2097156 | tf_op jit(solution)/shard_map/while/body/jit(dynamic_update_index_in_dim)/dynamic_update_slice | solution.py:237
  1071.2 28.4 %dynamic_update_slice.33 = f32[8,2048,128]{2,0,1:T(8,128)} dynamic-update-slice(f32[8,2048,128]{2,0,1:T(8,128)} %get-tuple-element.539, f32[1,2048,128]{2,0,1:T(1,128)S(1)} %bitcast.348, s32[]{:T(128)S(6)} %copy.84, s32[]{:T(128)} %constant.120.clone.1..sunk.1, s32[]{:T(128)} %constant.120.clone.1..sunk.1) | dynamic-update-slice | bytes 2097156 | tf_op jit(solution)/shard_map/while/body/jit(dynamic_update_index_in_dim)/dynamic_update_slice | solution.py:237
  1104.2 28.4 %dynamic_update_slice.34 = f32[8,2048,128]{2,0,1:T(8,128)} dynamic-update-slice(f32[8,2048,128]{2,0,1:T(8,128)} %get-tuple-element.540, f32[1,2048,128]{2,0,1:T(1,128)S(1)} %bitcast.347, s32[]{:T(128)S(6)} %copy.84, s32[]{:T(128)} %constant.120.clone.1..sunk.1, s32[]{:T(128)} %constant.120.clone.1..sunk.1) | dynamic-update-slice | bytes 2097156 | tf_op jit(solution)/shard_map/while/body/jit(dynamic_update_index_in_dim)/dynamic_update_slice | solution.py:237
  1154.7 28.4 %dynamic_update_slice.33 = f32[8,2048,128]{2,0,1:T(8,128)} dynamic-update-slice(f32[8,2048,128]{2,0,1:T(8,128)} %get-tuple-element.539, f32[1,2048,128]{2,0,1:T(1,128)S(1)} %bitcast.348, s32[]{:T(128)S(6)} %copy.84, s32[]{:T(128)} %constant.120.clone.1..sunk.1, s32[]{:T(128)} %constant.120.clone.1..sunk.1) | dynamic-update-slice | bytes 2097156 | tf_op jit(solution)/shard_map/while/body/jit(dynamic_update_index_in_dim)/dynamic_update_slice | solution.py:237
  1187.7 28.4 %dynamic_update_slice.34 = f32[8,2048,128]{2,0,1:T(8,128)} dynamic-update-slice(f32[8,2048,128]{2,0,1:T(8,128)} %get-tuple-element.540, f32[1,2048,128]{2,0,1:T(1,128)S(1)} %bitcast.347, s32[]{:T(128)S(6)} %copy.84, s32[]{:T(128)} %constant.120.clone.1..sunk.1, s32[]{:T(128)} %constant.120.clone.1..sunk.1) | dynamic-update-slice | bytes 2097156 | tf_op jit(solution)/shard_map/while/body/jit(dynamic_update_index_in_dim)/dynamic_update_slice | solution.py:237
  1238.2 28.4 %dynamic_update_slice.33 = f32[8,2048,128]{2,0,1:T(8,128)} dynamic-update-slice(f32[8,2048,128]{2,0,1:T(8,128)} %get-tuple-element.539, f32[1,2048,128]{2,0,1:T(1,128)S(1)} %bitcast.348, s32[]{:T(128)S(6)} %copy.84, s32[]{:T(128)} %constant.120.clone.1..sunk.1, s32[]{:T(128)} %constant.120.clone.1..sunk.1) | dynamic-update-slice | bytes 2097156 | tf_op jit(solution)/shard_map/while/body/jit(dynamic_update_index_in_dim)/dynamic_update_slice | solution.py:237
  1271.2 28.4 %dynamic_update_slice.34 = f32[8,2048,128]{2,0,1:T(8,128)} dynamic-update-slice(f32[8,2048,128]{2,0,1:T(8,128)} %get-tuple-element.540, f32[1,2048,128]{2,0,1:T(1,128)S(1)} %bitcast.347, s32[]{:T(128)S(6)} %copy.84, s32[]{:T(128)} %constant.120.clone.1..sunk.1, s32[]{:T(128)} %constant.120.clone.1..sunk.1) | dynamic-update-slice | bytes 2097156 | tf_op jit(solution)/shard_map/while/body/jit(dynamic_update_index_in_dim)/dynamic_update_slice | solution.py:237
  1321.7 28.4 %dynamic_update_slice.33 = f32[8,2048,128]{2,0,1:T(8,128)} dynamic-update-slice(f32[8,2048,128]{2,0,1:T(8,128)} %get-tuple-element.539, f32[1,2048,128]{2,0,1:T(1,128)S(1)} %bitcast.348, s32[]{:T(128)S(6)} %copy.84, s32[]{:T(128)} %constant.120.clone.1..sunk.1, s32[]{:T(128)} %constant.120.clone.1..sunk.1) | dynamic-update-slice | bytes 2097156 | tf_op jit(solution)/shard_map/while/body/jit(dynamic_update_index_in_dim)/dynamic_update_slice | solution.py:237
  1354.6 28.4 %dynamic_update_slice.34 = f32[8,2048,128]{2,0,1:T(8,128)} dynamic-update-slice(f32[8,2048,128]{2,0,1:T(8,128)} %get-tuple-element.540, f32[1,2048,128]{2,0,1:T(1,128)S(1)} %bitcast.347, s32[]{:T(128)S(6)} %copy.84, s32[]{:T(128)} %constant.120.clone.1..sunk.1, s32[]{:T(128)} %constant.120.clone.1..sunk.1) | dynamic-update-slice | bytes 2097156 | tf_op jit(solution)/shard_map/while/body/jit(dynamic_update_index_in_dim)/dynamic_update_slice | solution.py:237
  1405.1 28.4 %dynamic_update_slice.33 = f32[8,2048,128]{2,0,1:T(8,128)} dynamic-update-slice(f32[8,2048,128]{2,0,1:T(8,128)} %get-tuple-element.539, f32[1,2048,128]{2,0,1:T(1,128)S(1)} %bitcast.348, s32[]{:T(128)S(6)} %copy.84, s32[]{:T(128)} %constant.120.clone.1..sunk.1, s32[]{:T(128)} %constant.120.clone.1..sunk.1) | dynamic-update-slice | bytes 2097156 | tf_op jit(solution)/shard_map/while/body/jit(dynamic_update_index_in_dim)/dynamic_update_slice | solution.py:237
  1438.1 28.4 %dynamic_update_slice.34 = f32[8,2048,128]{2,0,1:T(8,128)} dynamic-update-slice(f32[8,2048,128]{2,0,1:T(8,128)} %get-tuple-element.540, f32[1,2048,128]{2,0,1:T(1,128)S(1)} %bitcast.347, s32[]{:T(128)S(6)} %copy.84, s32[]{:T(128)} %constant.120.clone.1..sunk.1, s32[]{:T(128)} %constant.120.clone.1..sunk.1) | dynamic-update-slice | bytes 2097156 | tf_op jit(solution)/shard_map/while/body/jit(dynamic_update_index_in_dim)/dynamic_update_slice | solution.py:237
  1481.5 82.9 %collective-permute-done.2 = f32[8,1024,128]{2,0,1:T(8,128)S(1)} collective-permute-done((f32[8,1024,128]{2,0,1:T(8,128)S(1)}, f32[8,1024,128]{2,0,1:T(8,128)S(1)}, u32[]{:S(2)}, u32[]{:S(2)}) %collective-permute-start.2) | collective-permute-done | bytes 4194336 | tf_op jit(solution)/shard_map/ppermute | solution.py:16
  1566.1 87.2 %collective-permute-done.3 = f32[8,1024,128]{2,0,1:T(8,128)S(1)} collective-permute-done((f32[8,1024,128]{2,0,1:T(8,128)S(1)}, f32[8,1024,128]{2,0,1:T(8,128)S(1)}, u32[]{:S(2)}, u32[]{:S(2)}) %collective-permute-start.3) | collective-permute-done | bytes 4194336 | tf_op jit(solution)/shard_map/ppermute | solution.py:16
  (455 shorter events, 487.4 us)
Async XLA Ops:
  286.5 7.1 copy-start.9
  286.5 335.4 %all-to-all-start.1 = ((bf16[8,5,128,8,128]{4,3,2,1,0:T(8,128)(2,1)}), bf16[8,5,128,8,128]{4,3,2,1,0:T(8,128)(2,1)}, u32[]{:S(2)}, u32[]{:S(2)}) async-start(bf16[8,5,128,8,128]{4,3,2,1,0:T(8,128)(2,1)} %get-tuple-element.282), calls=%async_computation.1 | async-start | bytes 20971520 | tf_op jit(solution)/shard_map/all_to_all | solution.py:43
  293.5 5.0 copy-start.10
  295.2 269.0 %collective-permute-start = (bf16[1024,8,128]{2,0,1:T(8,128)(2,1)}, bf16[1024,8,128]{2,0,1:T(8,128)(2,1)}, u32[]{:S(2)}, u32[]{:S(2)}) collective-permute-start(bf16[1024,8,128]{2,0,1:T(8,128)(2,1)} %copy.39), channel_id=1, source_target_pairs={{0,4},{4,8},{8,12},{12,16},{16,20},{20,24},{24,28},{1,5},{5,9},{9,... | collective-permute-start | bytes 6291464 | tf_op jit(solution)/shard_map/ppermute | solution.py:16
  298.8 310.2 %collective-permute-start.1 = (bf16[1024,8,128]{2,0,1:T(8,128)(2,1)S(1)}, bf16[1024,8,128]{2,0,1:T(8,128)(2,1)}, u32[]{:S(2)}, u32[]{:S(2)}) collective-permute-start(bf16[1024,8,128]{2,0,1:T(8,128)(2,1)S(1)} %copy.43), channel_id=1, source_target_pairs={{0,4},{4,8},{8,12},{12,16},{16,20},{20,24},{24,28},{1,5},{5,9},{9,... | collective-permute-start | bytes 6291464 | tf_op jit(solution)/shard_map/ppermute | solution.py:16
  820.0 29.2 %copy-start.8 = (bf16[1,1024,128]{2,1,0:T(8,128)(2,1)S(1)}, bf16[1,1024,128]{2,1,0:T(8,128)(2,1)}, u32[]{:S(2)}) copy-start(bf16[1,1024,128]{2,1,0:T(8,128)(2,1)} %copy-done.6) | copy-start | bytes 786436 | tf_op jit(solution)/shard_map/while
  886.1 4.3 copy-start.6
  903.5 29.2 %copy-start.8 = (bf16[1,1024,128]{2,1,0:T(8,128)(2,1)S(1)}, bf16[1,1024,128]{2,1,0:T(8,128)(2,1)}, u32[]{:S(2)}) copy-start(bf16[1,1024,128]{2,1,0:T(8,128)(2,1)} %copy-done.6) | copy-start | bytes 786436 | tf_op jit(solution)/shard_map/while
  969.5 4.3 copy-start.6
  986.9 29.2 %copy-start.8 = (bf16[1,1024,128]{2,1,0:T(8,128)(2,1)S(1)}, bf16[1,1024,128]{2,1,0:T(8,128)(2,1)}, u32[]{:S(2)}) copy-start(bf16[1,1024,128]{2,1,0:T(8,128)(2,1)} %copy-done.6) | copy-start | bytes 786436 | tf_op jit(solution)/shard_map/while
  1053.0 4.3 copy-start.6
  1070.4 29.2 %copy-start.8 = (bf16[1,1024,128]{2,1,0:T(8,128)(2,1)S(1)}, bf16[1,1024,128]{2,1,0:T(8,128)(2,1)}, u32[]{:S(2)}) copy-start(bf16[1,1024,128]{2,1,0:T(8,128)(2,1)} %copy-done.6) | copy-start | bytes 786436 | tf_op jit(solution)/shard_map/while
  1153.9 29.2 %copy-start.8 = (bf16[1,1024,128]{2,1,0:T(8,128)(2,1)S(1)}, bf16[1,1024,128]{2,1,0:T(8,128)(2,1)}, u32[]{:S(2)}) copy-start(bf16[1,1024,128]{2,1,0:T(8,128)(2,1)} %copy-done.6) | copy-start | bytes 786436 | tf_op jit(solution)/shard_map/while
  1237.3 29.2 %copy-start.8 = (bf16[1,1024,128]{2,1,0:T(8,128)(2,1)S(1)}, bf16[1,1024,128]{2,1,0:T(8,128)(2,1)}, u32[]{:S(2)}) copy-start(bf16[1,1024,128]{2,1,0:T(8,128)(2,1)} %copy-done.6) | copy-start | bytes 786436 | tf_op jit(solution)/shard_map/while
  1320.8 29.2 %copy-start.8 = (bf16[1,1024,128]{2,1,0:T(8,128)(2,1)S(1)}, bf16[1,1024,128]{2,1,0:T(8,128)(2,1)}, u32[]{:S(2)}) copy-start(bf16[1,1024,128]{2,1,0:T(8,128)(2,1)} %copy-done.6) | copy-start | bytes 786436 | tf_op jit(solution)/shard_map/while
  1404.3 29.2 %copy-start.8 = (bf16[1,1024,128]{2,1,0:T(8,128)(2,1)S(1)}, bf16[1,1024,128]{2,1,0:T(8,128)(2,1)}, u32[]{:S(2)}) copy-start(bf16[1,1024,128]{2,1,0:T(8,128)(2,1)} %copy-done.6) | copy-start | bytes 786436 | tf_op jit(solution)/shard_map/while
  1466.5 97.9 %slice-start = ((s8[8388608]{0:T(1024)(128)(4,1)}), s8[4194304]{0:T(1024)(128)(4,1)S(1)}, s32[]{:S(2)}) async-start(s8[8388608]{0:T(1024)(128)(4,1)} %bitcast.359), calls=%async_computation.3 | async-start | bytes 8388608
  1469.1 95.3 %collective-permute-start.2 = (f32[8,1024,128]{2,0,1:T(8,128)S(1)}, f32[8,1024,128]{2,0,1:T(8,128)S(1)}, u32[]{:S(2)}, u32[]{:S(2)}) collective-permute-start(f32[8,1024,128]{2,0,1:T(8,128)S(1)} %slice.47), channel_id=1, source_target_pairs={{4,0},{8,4},{12,8},{16,12},{20,16},{24,20},{28,24},{5,1},{9,5},{13... | collective-permute-start | bytes 12582920 | tf_op jit(solution)/shard_map/ppermute | solution.py:16
  1471.0 5.1 copy-start.4
  1471.0 93.4 %slice-start.1 = ((s8[8388608]{0:T(1024)(128)(4,1)}), s8[4194304]{0:T(1024)(128)(4,1)S(1)}, s32[]{:S(2)}) async-start(s8[8388608]{0:T(1024)(128)(4,1)} %bitcast.359), calls=%async_computation.4 | async-start | bytes 8388608
  1473.6 5.2 copy-start.5
  1473.7 179.7 %collective-permute-start.3 = (f32[8,1024,128]{2,0,1:T(8,128)S(1)}, f32[8,1024,128]{2,0,1:T(8,128)S(1)}, u32[]{:S(2)}, u32[]{:S(2)}) collective-permute-start(f32[8,1024,128]{2,0,1:T(8,128)S(1)} %slice.49), channel_id=1, source_target_pairs={{4,0},{8,4},{12,8},{16,12},{20,16},{24,20},{28,24},{5,1},{9,5},{13... | collective-permute-start | bytes 12582920 | tf_op jit(solution)/shard_map/ppermute | solution.py:16
  1476.1 177.2 %slice-start.2 = ((s8[8388608]{0:T(1024)(128)(4,1)}), s8[4194304]{0:T(1024)(128)(4,1)S(1)}, s32[]{:S(2)}) async-start(s8[8388608]{0:T(1024)(128)(4,1)} %bitcast.361), calls=%async_computation.5 | async-start | bytes 8388608
  1481.5 171.9 %slice-start.3 = ((s8[8388608]{0:T(1024)(128)(4,1)}), s8[4194304]{0:T(1024)(128)(4,1)S(1)}, s32[]{:S(2)}) async-start(s8[8388608]{0:T(1024)(128)(4,1)} %bitcast.361), calls=%async_computation.6 | async-start | bytes 8388608
  (45 other events, 135.9 us)
where the time goes:
time: 1670 us; the launch traced here: 1660 us
  local copies, waits for them, and re-layouts  544 us (33%)
  waiting for transfers between devices  467 us (28%)
  matrix products  302 us (18%)
  blocking collectives  251 us (15%)
  other arithmetic  69.5 us (4%)
  starting transfers between devices  18.3 us (1%)
    ppermute x4, waiting for transfers between devices, passed_along(): return lax.ppermute(block, axis, route)  467 us
    dynamic_update_slice x16, local copies, waits for them, and re-layouts, shards(): lax.map(backward_head, (queries_major, grads_major, keys_major, values_ma...  454 us
    all_to_all x1, blocking collectives, fetch_memory(): lax.all_to_all(jnp.take(value_blocks, wanted, axis=0), 'seq', split_axis=...  231 us
    dot_general x16, matrix products, score_parts(): jnp.einsum('twd,tjd->twj', query_tiles, key_tiles[:-1], preferred_element...  43.1 us
    dot_general x16, matrix products, mix(): jnp.einsum('twj,tjd->twd', lower_w, key_tiles[:-1], preferred_element_typ...  36.3 us
    dot_general x16, matrix products, mix(): jnp.einsum('nbm,nmd->nbd', far_w, mem_rows, preferred_element_type=jnp.fl...  34.1 us
  transfers between devices with their start and end apart: 5, of which 4 were waited for; matrix products, arithmetic and copies ran while one was open for 2% of the time, Pallas kernels for 0%

commit v1 on v0

v1 whole, which is shorter than its diff:
```python
import math

import jax
import jax.numpy as jnp
from jax import lax
from jax.experimental import pallas as pl
from jax.experimental.pallas import tpu as pltpu
from jax.sharding import PartitionSpec as P

WINDOW = 1024
BLOCK = 128
TOPK = 4
MASKED = -1e30
NT = (((1,), (1,)), ((), ()))
TN = (((0,), (0,)), ((), ()))
LOG2E = 1.4426950408889634


def dot(a, b, dims=(((1,), (0,)), ((), ()))):
    return lax.dot_general(a, b, dims, preferred_element_type=jnp.float32)


def attention_kernel(
    slot_ref, count_ref, first_ref, q_ref, g_ref, prev_ref, own_ref, mem_ref,
    o_ref, dq_ref, back_ref, dk_ref, dv_ref, kx, vx, dkx, dvx,
):
    tokens, head_dim = q_ref.shape
    span = WINDOW + BLOCK
    scale = 1.0 / math.sqrt(head_dim)
    kx[:WINDOW] = prev_ref[0]
    kx[WINDOW:] = own_ref[0]
    vx[:WINDOW] = prev_ref[1]
    vx[WINDOW:] = own_ref[1]
    dkx[...] = jnp.zeros_like(dkx)
    dvx[...] = jnp.zeros_like(dvx)
    start_col = first_ref[0] * WINDOW
    row = lax.broadcasted_iota(jnp.int32, (BLOCK, span), 0)
    col = lax.broadcasted_iota(jnp.int32, (BLOCK, span), 1)
    gap = col - row

    def block_step(b, carry):
        r0 = pl.multiple_of(b * BLOCK, BLOCK)
        rows = pl.ds(r0, BLOCK)
        window = pl.ds(r0, span)
        q = q_ref[rows, :]
        g = g_ref[rows, :]
        kw = kx[window, :]
        vw = vx[window, :]
        seen = (gap > 0) & (gap <= WINDOW) & (col >= start_col - r0)
        s = jnp.where(seen, dot(q, kw, NT) * (scale * LOG2E), MASKED)
        used = count_ref[b]
        km, vm, sm = [], [], []
        top = jnp.max(s, 1, keepdims=True)
        for i in range(TOPK):
            slot = slot_ref[b * TOPK + i]
            km.append(mem_ref[slot, 0])
            vm.append(mem_ref[slot, 1])
            far = dot(q, km[i], NT) * (scale * LOG2E)
            sm.append(jnp.where(i < used, far, MASKED))
            top = jnp.maximum(top, jnp.max(sm[i], 1, keepdims=True))
        p = jnp.exp2(s - top)
        total = jnp.sum(p, 1, keepdims=True)
        pm = []
        for i in range(TOPK):
            pm.append(jnp.exp2(sm[i] - top))
            total = total + jnp.sum(pm[i], 1, keepdims=True)
        inv = 1.0 / total
        p = p * inv
        pb = p.astype(jnp.bfloat16)
        o = dot(pb, vw)
        for i in range(TOPK):
            pm[i] = pm[i] * inv
            o = o + dot(pm[i].astype(jnp.bfloat16), vm[i])
        o = o.astype(jnp.bfloat16)
        o_ref[rows, :] = o
        delta = jnp.sum(g.astype(jnp.float32) * o.astype(jnp.float32), 1, keepdims=True)
        ds = (p * (dot(g, vw, NT) - delta)).astype(jnp.bfloat16)
        dq = dot(ds, kw)
        for i in range(TOPK):
            dsm = (pm[i] * (dot(g, vm[i], NT) - delta)).astype(jnp.bfloat16)
            dq = dq + dot(dsm, km[i])
        dq_ref[rows, :] = (dq * scale).astype(jnp.bfloat16)
        dkx[window, :] += dot(ds, q, TN)
        dvx[window, :] += dot(pb, g, TN)
        return carry

    lax.fori_loop(0, tokens // BLOCK, block_step, 0)
    back_ref[0] = (dkx[:WINDOW] * scale).astype(jnp.bfloat16)
    back_ref[1] = dvx[:WINDOW].astype(jnp.bfloat16)
    dk_ref[...] = dkx[WINDOW:] * scale
    dv_ref[...] = dvx[WINDOW:]


def attend(slots, counts, first, q, g, prev, own, mem):
    tokens, head_dim = q.shape
    ext = tokens + WINDOW
    vm = pl.BlockSpec(memory_space=pltpu.VMEM)
    sm = pl.BlockSpec(memory_space=pltpu.SMEM)
    row16 = jax.ShapeDtypeStruct((tokens, head_dim), jnp.bfloat16)
    row32 = jax.ShapeDtypeStruct((tokens, head_dim), jnp.float32)
    flops = 2 * tokens * head_dim * (6 * (WINDOW + BLOCK) + 4 * TOPK * BLOCK)
    return pl.pallas_call(
        attention_kernel,
        out_shape=(row16, row16, jax.ShapeDtypeStruct((2, WINDOW, head_dim), jnp.bfloat16), row32, row32),
        in_specs=[sm] * 3 + [vm] * 5,
        out_specs=[vm] * 5,
        scratch_shapes=[
            pltpu.VMEM((ext, head_dim), jnp.bfloat16),
            pltpu.VMEM((ext, head_dim), jnp.bfloat16),
            pltpu.VMEM((ext, head_dim), jnp.float32),
            pltpu.VMEM((ext, head_dim), jnp.float32),
        ],
        compiler_params=pltpu.CompilerParams(vmem_limit_bytes=32 << 20),
        cost_estimate=pl.CostEstimate(flops=flops, bytes_accessed=6 << 20, transcendentals=tokens * 1664),
        name="attend",
    )(slots, counts, first, q, g, prev, own, mem)


def shards(queries, seg_keys, seg_values, mem_keys, mem_values, mem_blocks, mem_count, grad_out):
    tokens, heads, head_dim = queries.shape
    owners = lax.axis_size("seq")
    rank = lax.axis_index("seq")
    n_blocks = tokens // BLOCK
    mem_local = mem_keys.shape[0] // BLOCK
    live_total = n_blocks * (TOPK + 1) // 2
    cap = max(2, 2 * live_total // owners)
    along = [(i, i + 1) for i in range(owners - 1)]
    back = [(i + 1, i) for i in range(owners - 1)]

    packed = jnp.concatenate([mem_blocks, mem_count[:, None]], 1)
    packed = lax.all_gather(packed, ("seq", "head"), axis=0, tiled=True)
    ids = packed[:, :TOPK].reshape(owners, n_blocks * TOPK)
    counts = packed[:, TOPK].reshape(owners, n_blocks)
    live = (jnp.arange(TOPK, dtype=jnp.int32)[None, None, :] < counts[:, :, None]).reshape(owners, -1)
    owner_of = ids // mem_local
    hot = (owner_of[:, :, None] == jnp.arange(owners, dtype=jnp.int32)) & live[:, :, None]
    order = jnp.sum((jnp.cumsum(hot.astype(jnp.int32), 1) - 1) * hot, 2)
    mine = (owner_of == rank) & live
    pick = mine[:, :, None] & (order[:, :, None] == jnp.arange(cap, dtype=jnp.int32))
    send_idx = jnp.sum(jnp.where(pick, (ids % mem_local)[:, :, None], 0), 1)
    send_idx = jnp.roll(send_idx, -rank, 0)
    slots = jnp.where(live, ((rank - owner_of) % owners) * cap + order, 0)
    slots = lax.dynamic_index_in_dim(slots, rank, 0, keepdims=False)
    my_counts = lax.dynamic_index_in_dim(counts, rank, 0, keepdims=False)
    first = (rank == 0).astype(jnp.int32)[None]

    q_major = jnp.moveaxis(queries, 1, 0)
    g_major = jnp.moveaxis(grad_out, 1, 0)
    kv_major = jnp.stack([jnp.moveaxis(seg_keys, 1, 0), jnp.moveaxis(seg_values, 1, 0)], 1)
    mem_major = jnp.stack(
        [
            jnp.moveaxis(m.reshape(mem_local, BLOCK, heads, head_dim), 2, 0)
            for m in (mem_keys, mem_values)
        ],
        2,
    )
    arrived, outs = [], []
    for h in range(heads):
        own = kv_major[h]
        send = mem_major[h][send_idx]
        if h >= 2:
            own, send, _ = lax.optimization_barrier((own, send, arrived[h - 2]))
        prev = lax.ppermute(own, "seq", along)
        parts = [send[0]] + [
            lax.ppermute(send[d], "seq", [(i, (i + d) % owners) for i in range(owners)])
            for d in range(1, owners)
        ]
        arrived.append((prev, parts))
    for h in range(heads):
        prev, parts = arrived[h]
        mem = jnp.concatenate(parts, 0)
        o, dq, ret, dk, dv = attend(slots, my_counts, first, q_major[h], g_major[h], prev, kv_major[h], mem)
        ret = lax.ppermute(ret, "seq", back).astype(jnp.float32)
        outs.append((o, dq, (dk + ret[0]).astype(jnp.bfloat16), (dv + ret[1]).astype(jnp.bfloat16)))
    return tuple(jnp.stack([o[i] for o in outs], 1) for i in range(4))


def solution(mesh):
    rows = P("seq", "head", None)
    return jax.shard_map(
        shards,
        mesh=mesh,
        in_specs=(rows, rows, rows, rows, rows, P(("seq", "head"), None), P(("seq", "head")), rows),
        out_specs=(rows, rows, rows, rows),
        check_vma=False,
    )
```

time: 1670 us -> 729 us (0.44)
  local copies, waits for them, and re-layouts: 544 us -> 89.4 us
  matrix products: 302 us -> 0 us
  waiting for transfers between devices: 467 us -> 201 us
  starting transfers between devices: 18.3 us -> 268 us
  blocking collectives: 251 us -> 31.4 us
  other arithmetic: 69.5 us -> 111 us
    dynamic_update_slice x24 -> x0, local copies, waits for them, and re-layouts: 455 us -> none  [the longest x16 454 us: shards(): lax.map(backward_head, (queries_major, grads_major, keys_major, values_ma...]
    dot_general x144 -> x0, matrix products: 302 us -> none  [the longest x16 43.1 us: score_parts(): jnp.einsum('twd,tjd->twj', query_tiles, key_tiles[:-1], preferred_element...]
    ppermute x4 -> x72, waiting for transfers between devices: 467 us -> 201 us  [the longest x56 170 us: shards(): lax.ppermute(send[d], 'seq', [(i, (i + d) % owners) for i in range(owners)])]
    ppermute x4 -> x72, starting transfers between devices: 11.3 us -> 268 us  [the longest x56 203 us: shards(): lax.ppermute(send[d], 'seq', [(i, (i + d) % owners) for i in range(owners)])]
    all_to_all x2 -> x0, blocking collectives: 241 us -> none  [the longest x1 231 us: fetch_memory(): lax.all_to_all(jnp.take(value_blocks, wanted, axis=0), 'seq', split_axis=...]
    pallas_call x0 -> x7, other arithmetic: none -> 94.1 us  [attend(): pl.pallas_call(attention_kernel, out_shape=(row16, row16, jax.ShapeDtypeS...]
    reduce_sum x25 -> x1, other arithmetic: 41.7 us -> 0.19 us  [shards(): send_idx = jnp.sum(jnp.where(pick, (ids % mem_local)[:, :, None], 0), 1)]
    unnamed x21 -> x150, local copies, waits for them, and re-layouts: 4.07 us -> 44.9 us
  transfers between devices with their start and end apart: 5 -> 72, of which waited for: 4 -> 23; matrix products, arithmetic and copies ran while one was open for 2% -> 21% of each run, Pallas kernels for 0% -> 0%
where the time goes in v1:
time: 729 us; the launch traced here: 718 us
  starting transfers between devices  268 us (37%)
  waiting for transfers between devices  201 us (28%)
  other arithmetic  111 us (15%)
  local copies, waits for them, and re-layouts  89.4 us (12%)
  blocking collectives  31.4 us (4%)
  Pallas kernels  13.4 us (2%)
    ppermute x56, starting transfers between devices, shards(): lax.ppermute(send[d], 'seq', [(i, (i + d) % owners) for i in range(owners)])  203 us
    ppermute x56, waiting for transfers between devices, shards(): lax.ppermute(send[d], 'seq', [(i, (i + d) % owners) for i in range(owners)])  170 us
    pallas_call x7, other arithmetic, attend(): pl.pallas_call(attention_kernel, out_shape=(row16, row16, jax.ShapeDtypeS...  94.1 us
    unnamed x150, local copies, waits for them, and re-layouts  44.9 us
    ppermute x8, starting transfers between devices, shards(): prev = lax.ppermute(own, 'seq', along)  35.4 us
    all_gather x1, blocking collectives, shards(): packed = lax.all_gather(packed, ('seq', 'head'), axis=0, tiled=True)  31.4 us
    gather x8, local copies, waits for them, and re-layouts, shards(): send = mem_major[h][send_idx]  31.4 us
    ppermute x8, starting transfers between devices, shards(): ret = lax.ppermute(ret, 'seq', back).astype(jnp.float32)  30.3 us
  transfers between devices with their start and end apart: 72, of which 23 were waited for; matrix products, arithmetic and copies ran while one was open for 21% of the time, Pallas kernels for 0%

profile of v1, /device:TPU:16, one launch (start us, length us, event | category | flops | bytes accessed | tf_op | source)
XLA Modules:
  0.0 717.5 jit_solution(9757772039773357757)
XLA Ops:
  2.1 31.4 %all-gather = s32[32,2,5]{2,1,0:T(2,128)S(1)} all-gather(s32[1,2,5]{2,1,0:T(2,128)S(1)} %add_bitcast_fusion), channel_id=1, replica_groups=mesh['seq'=8,'head'=4] {'seq','head'}, dimensions={0}, use_global_device_ids=true | all-gather | bytes 1320 | tf_op jit(solution)/shard_map/all_gather | solution.py:131
  51.4 10.7 %fusion.7 = (bf16[32,2,128,128]{3,2,1,0:T(8,128)(2,1)S(1)}, bf16[32,2,128,128]{3,2,1,0:T(8,128)(2,1)}, bf16[32,2,128,128]{3,2,1,0:T(8,128)(2,1)}, bf16[32,2,128,...) fusion(bf16[8,32,1,128,128]{4,3,2,1,0:T(8,128)(2,1)} %bitcast.4, ...), kind=kLoop, calls=%fused_computation.44 | loop fusion | flops 8388608 | bytes 33554432 | tf_op jit(solution)/shard_map/squeeze | solution.py:160
  154.9 11.2 %collective-permute-done.9 = bf16[5,2,128,128]{3,2,1,0:T(8,128)(2,1)S(1)} collective-permute-done((bf16[5,2,128,128]{3,2,1,0:T(8,128)(2,1)}, bf16[5,2,128,128]{3,2,1,0:T(8,128)(2,1)S(1)}, u32[]{:S(2)}, u32[]{:S(2)}) %collective-permute-start.9) | collective-permute-done | bytes 327712 | tf_op jit(solution)/shard_map/ppermute | solution.py:165
  172.9 27.8 %collective-permute-start.15 = (bf16[5,2,128,128]{3,2,1,0:T(8,128)(2,1)S(1)}, bf16[5,2,128,128]{3,2,1,0:T(8,128)(2,1)S(1)}, u32[]{:S(2)}, u32[]{:S(2)}) collective-permute-start(bf16[5,2,128,128]{3,2,1,0:T(8,128)(2,1)S(1)} %get-tuple-element.259), channel_id=1, source_target_pairs={{0,28},{4,0},{8,4},{12,8},{16,12},{20,16},{24,20},{28,24},{1,29},{... | collective-permute-start | bytes 983048 | tf_op jit(solution)/shard_map/ppermute | solution.py:165
  205.5 11.3 %collective-permute-done.8 = bf16[2,1024,128]{2,1,0:T(8,128)(2,1)S(1)} collective-permute-done((bf16[2,1024,128]{2,1,0:T(8,128)(2,1)S(1)}, bf16[2,1024,128]{2,1,0:T(8,128)(2,1)S(1)}, u32[]{:S(2)}, u32[]{:S(2)}) %collective-permute-start.8) | collective-permute-done | bytes 524320 | tf_op jit(solution)/shard_map/ppermute | solution.py:163
  218.5 13.4 %attend.8 = (bf16[1024,128]{1,0:T(8,128)(2,1)S(1)}, bf16[1024,128]{1,0:T(8,128)(2,1)S(1)}, bf16[2,1024,128]{2,1,0:T(8,128)(2,1)S(1)}, f32[1024,128]{1,0:T(8,128)S(1)}, f32[1024,128]{1,0:T(8,128)S(1)}) custom-call(s32[32]{0:T(128)S(1)} %fusion.105.slot_ref, s32[8]{0:T(128)S(1)} %fusion.108.count_ref, s32[1]{0:T(128)} %bitcast.5.first_ref, ...), custom_call_target="tpu_custom_call" | custom-call | flops 2348810240 | bytes 6291456 | tf_op jit(solution)/shard_map/attend/pallas_call | solution.py:102
  244.2 13.4 %attend.15 = (bf16[1024,8,128]{2,0,1:T(8,128)(2,1)S(1)}, bf16[1024,128]{1,0:T(8,128)(2,1)S(1)}, f32[1024,128]{1,0:T(8,128)S(1)}, bf16[2,1024,128]{2,1,0:T(8,128)(2,1)S(1)}, f32[1024,128]{1,0:T(8,128)S(1)}) fusion(bf16[1024,8,128]{2,0,1:T(8,128)(2,1)S(1)} %bitcast_dynamic-update-slice_fusion.17, s32[32]{0:T(128)S(1)} %fusion.105.slot_ref, ...), kind=kCustom, calls=%fused_computation.232 | custom fusion | flops 2348810240 | bytes 6292484 | tf_op jit(solution)/shard_map/attend/pallas_call | solution.py:102
  260.9 29.4 %collective-permute-start.23 = (bf16[5,2,128,128]{3,2,1,0:T(8,128)(2,1)S(1)}, bf16[5,2,128,128]{3,2,1,0:T(8,128)(2,1)S(1)}, u32[]{:S(2)}, u32[]{:S(2)}) collective-permute-start(bf16[5,2,128,128]{3,2,1,0:T(8,128)(2,1)S(1)} %get-tuple-element.252), channel_id=1, source_target_pairs={{0,28},{4,0},{8,4},{12,8},{16,12},{20,16},{24,20},{28,24},{1,29},{... | collective-permute-start | bytes 983048 | tf_op jit(solution)/shard_map/ppermute | solution.py:165
  295.9 13.1 %collective-permute-done.22 = bf16[5,2,128,128]{3,2,1,0:T(8,128)(2,1)S(1)} collective-permute-done((bf16[5,2,128,128]{3,2,1,0:T(8,128)(2,1)S(1)}, bf16[5,2,128,128]{3,2,1,0:T(8,128)(2,1)S(1)}, u32[]{:S(2)}, u32[]{:S(2)}) %collective-permute-start.22) | collective-permute-done | bytes 327712 | tf_op jit(solution)/shard_map/ppermute | solution.py:165
  316.2 25.1 %collective-permute-done.25 = bf16[5,2,128,128]{3,2,1,0:T(8,128)(2,1)S(1)} collective-permute-done((bf16[5,2,128,128]{3,2,1,0:T(8,128)(2,1)S(1)}, bf16[5,2,128,128]{3,2,1,0:T(8,128)(2,1)S(1)}, u32[]{:S(2)}, u32[]{:S(2)}) %collective-permute-start.25) | collective-permute-done | bytes 327712 | tf_op jit(solution)/shard_map/ppermute | solution.py:165
  350.8 10.6 %collective-permute-start.31 = (bf16[5,2,128,128]{3,2,1,0:T(8,128)(2,1)S(1)}, bf16[5,2,128,128]{3,2,1,0:T(8,128)(2,1)S(1)}, u32[]{:S(2)}, u32[]{:S(2)}) collective-permute-start(bf16[5,2,128,128]{3,2,1,0:T(8,128)(2,1)S(1)} %get-tuple-element.245), channel_id=1, source_target_pairs={{0,28},{4,0},{8,4},{12,8},{16,12},{20,16},{24,20},{28,24},{1,29},{... | collective-permute-start | bytes 983048 | tf_op jit(solution)/shard_map/ppermute | solution.py:165
  371.1 13.4 %attend.14 = (bf16[1024,8,128]{2,0,1:T(8,128)(2,1)S(1)}, bf16[1024,128]{1,0:T(8,128)(2,1)S(1)}, f32[1024,128]{1,0:T(8,128)S(1)}, bf16[2,1024,128]{2,1,0:T(8,128)(2,1)S(1)}, f32[1024,128]{1,0:T(8,128)S(1)}) fusion(bf16[1024,8,128]{2,0,1:T(8,128)(2,1)S(1)} %get-tuple-element.150, s32[32]{0:T(128)S(1)} %fusion.105.slot_ref, s32[8]{0:T(128)S(1)} %fusion.108.count_ref, ...), kind=kCustom, calls=%fused_computation.231 | custom fusion | flops 2348810240 | bytes 6292484 | tf_op jit(solution)/shard_map/attend/pallas_call | solution.py:102
  384.5 11.8 %collective-permute-start.66 = (bf16[2,1024,128]{2,1,0:T(8,128)(2,1)S(1)}, bf16[2,1024,128]{2,1,0:T(8,128)(2,1)S(1)}, u32[]{:S(2)}, u32[]{:S(2)}) collective-permute-start(bf16[2,1024,128]{2,1,0:T(8,128)(2,1)S(1)} %get-tuple-element.145), channel_id=1, source_target_pairs={{4,0},{8,4},{12,8},{16,12},{20,16},{24,20},{28,24},{5,1},{9,5},{13... | collective-permute-start | bytes 1572872 | tf_op jit(solution)/shard_map/ppermute | solution.py:173
  408.5 13.4 %attend.13 = (bf16[1024,8,128]{2,0,1:T(8,128)(2,1)S(1)}, bf16[1024,128]{1,0:T(8,128)(2,1)S(1)}, f32[1024,128]{1,0:T(8,128)S(1)}, bf16[2,1024,128]{2,1,0:T(8,128)(2,1)S(1)}, f32[1024,128]{1,0:T(8,128)S(1)}) fusion(bf16[1024,8,128]{2,0,1:T(8,128)(2,1)S(1)} %get-tuple-element.140, s32[32]{0:T(128)S(1)} %fusion.105.slot_ref, s32[8]{0:T(128)S(1)} %fusion.108.count_ref, ...), kind=kCustom, calls=%fused_computation.230 | custom fusion | flops 2348810240 | bytes 6292484 | tf_op jit(solution)/shard_map/attend/pallas_call | solution.py:102
  425.2 22.2 %collective-permute-start.39 = (bf16[5,2,128,128]{3,2,1,0:T(8,128)(2,1)S(1)}, bf16[5,2,128,128]{3,2,1,0:T(8,128)(2,1)S(1)}, u32[]{:S(2)}, u32[]{:S(2)}) collective-permute-start(bf16[5,2,128,128]{3,2,1,0:T(8,128)(2,1)S(1)} %get-tuple-element.238), channel_id=1, source_target_pairs={{0,28},{4,0},{8,4},{12,8},{16,12},{20,16},{24,20},{28,24},{1,29},{... | collective-permute-start | bytes 983048 | tf_op jit(solution)/shard_map/ppermute | solution.py:165
  468.8 32.0 %collective-permute-done.41 = bf16[5,2,128,128]{3,2,1,0:T(8,128)(2,1)S(1)} collective-permute-done((bf16[5,2,128,128]{3,2,1,0:T(8,128)(2,1)S(1)}, bf16[5,2,128,128]{3,2,1,0:T(8,128)(2,1)S(1)}, u32[]{:S(2)}, u32[]{:S(2)}) %collective-permute-start.41) | collective-permute-done | bytes 327712 | tf_op jit(solution)/shard_map/ppermute | solution.py:165
  511.6 9.9 %collective-permute-start.47 = (bf16[5,2,128,128]{3,2,1,0:T(8,128)(2,1)S(1)}, bf16[5,2,128,128]{3,2,1,0:T(8,128)(2,1)S(1)}, u32[]{:S(2)}, u32[]{:S(2)}) collective-permute-start(bf16[5,2,128,128]{3,2,1,0:T(8,128)(2,1)S(1)} %get-tuple-element.231), channel_id=1, source_target_pairs={{0,28},{4,0},{8,4},{12,8},{16,12},{20,16},{24,20},{28,24},{1,29},{... | collective-permute-start | bytes 983048 | tf_op jit(solution)/shard_map/ppermute | solution.py:165
  555.2 9.9 %collective-permute-done.67 = bf16[2,1024,128]{2,1,0:T(8,128)(2,1)S(1)} collective-permute-done((bf16[2,1024,128]{2,1,0:T(8,128)(2,1)S(1)}, bf16[2,1024,128]{2,1,0:T(8,128)(2,1)S(1)}, u32[]{:S(2)}, u32[]{:S(2)}) %collective-permute-start.67) | collective-permute-done | bytes 524320 | tf_op jit(solution)/shard_map/ppermute | solution.py:173
  565.4 13.4 %attend.12 = (bf16[1024,8,128]{2,0,1:T(8,128)(2,1)S(1)}, bf16[1024,128]{1,0:T(8,128)(2,1)S(1)}, f32[1024,128]{1,0:T(8,128)S(1)}, bf16[2,1024,128]{2,1,0:T(8,128)(2,1)S(1)}, f32[1024,128]{1,0:T(8,128)S(1)}) fusion(bf16[1024,8,128]{2,0,1:T(8,128)(2,1)S(1)} %get-tuple-element.160, s32[32]{0:T(128)S(1)} %fusion.105.slot_ref, s32[8]{0:T(128)S(1)} %fusion.108.count_ref, ...), kind=kCustom, calls=%fused_computation.229 | custom fusion | flops 2348810240 | bytes 6292484 | tf_op jit(solution)/shard_map/attend/pallas_call | solution.py:102
  579.0 13.4 %attend.11 = (bf16[1024,8,128]{2,0,1:T(8,128)(2,1)S(1)}, bf16[1024,128]{1,0:T(8,128)(2,1)S(1)}, f32[1024,128]{1,0:T(8,128)S(1)}, bf16[2,1024,128]{2,1,0:T(8,128)(2,1)S(1)}, f32[1024,128]{1,0:T(8,128)S(1)}) fusion(bf16[1024,8,128]{2,0,1:T(8,128)(2,1)S(1)} %get-tuple-element.130, s32[32]{0:T(128)S(1)} %fusion.105.slot_ref, s32[8]{0:T(128)S(1)} %fusion.108.count_ref, ...), kind=kCustom, calls=%fused_computation.228 | custom fusion | flops 2348810240 | bytes 6292484 | tf_op jit(solution)/shard_map/attend/pallas_call | solution.py:102
  609.0 19.8 %collective-permute-done.57 = bf16[5,2,128,128]{3,2,1,0:T(8,128)(2,1)S(1)} collective-permute-done((bf16[5,2,128,128]{3,2,1,0:T(8,128)(2,1)S(1)}, bf16[5,2,128,128]{3,2,1,0:T(8,128)(2,1)S(1)}, u32[]{:S(2)}, u32[]{:S(2)}) %collective-permute-start.57) | collective-permute-done | bytes 327712 | tf_op jit(solution)/shard_map/ppermute | solution.py:165
  630.5 19.3 %collective-permute-start.56 = (bf16[2,1024,128]{2,1,0:T(8,128)(2,1)S(1)}, bf16[2,1024,128]{2,1,0:T(8,128)(2,1)S(1)}, u32[]{:S(2)}, u32[]{:S(2)}) collective-permute-start(bf16[2,1024,128]{2,1,0:T(8,128)(2,1)S(1)} %copy-done.13), channel_id=1, source_target_pairs={{0,4},{4,8},{8,12},{12,16},{16,20},{20,24},{24,28},{1,5},{5,9},{9,... | collective-permute-start | bytes 1572872 | tf_op jit(solution)/shard_map/ppermute | solution.py:163
  671.6 13.4 %attend.10 = (bf16[1024,8,128]{2,0,1:T(8,128)(2,1)S(1)}, bf16[1024,128]{1,0:T(8,128)(2,1)S(1)}, f32[1024,128]{1,0:T(8,128)S(1)}, bf16[2,1024,128]{2,1,0:T(8,128)(2,1)S(1)}, f32[1024,128]{1,0:T(8,128)S(1)}) fusion(bf16[1024,8,128]{2,0,1:T(8,128)(2,1)S(1)} %get-tuple-element.170, s32[32]{0:T(128)S(1)} %fusion.105.slot_ref, s32[8]{0:T(128)S(1)} %fusion.108.count_ref, ...), kind=kCustom, calls=%fused_computation.227 | custom fusion | flops 2348810240 | bytes 6292484 | tf_op jit(solution)/shard_map/attend/pallas_call | solution.py:102
  687.0 13.4 %attend.9 = (bf16[1024,8,128]{2,0,1:T(8,128)(2,1)S(1)}, bf16[1024,128]{1,0:T(8,128)(2,1)S(1)}, f32[1024,128]{1,0:T(8,128)S(1)}, bf16[2,1024,128]{2,1,0:T(8,128)(2,1)S(1)}, f32[1024,128]{1,0:T(8,128)S(1)}) fusion(bf16[1024,8,128]{2,0,1:T(8,128)(2,1)S(1)} %get-tuple-element.180, s32[32]{0:T(128)S(1)} %fusion.105.slot_ref, s32[8]{0:T(128)S(1)} %fusion.108.count_ref, ...), kind=kCustom, calls=%fused_computation.226 | custom fusion | flops 2348810240 | bytes 6292484 | tf_op jit(solution)/shard_map/attend/pallas_call | solution.py:102
  (349 shorter events, 312.0 us)
Async XLA Ops:
  69.5 56.7 %collective-permute-start.1 = (bf16[5,2,128,128]{3,2,1,0:T(8,128)(2,1)}, bf16[5,2,128,128]{3,2,1,0:T(8,128)(2,1)}, u32[]{:S(2)}, u32[]{:S(2)}) collective-permute-start(bf16[5,2,128,128]{3,2,1,0:T(8,128)(2,1)} %get-tuple-element.273), channel_id=1, source_target_pairs={{0,4},{4,8},{8,12},{12,16},{16,20},{20,24},{24,28},{28,0},{1,5},{5... | collective-permute-start | bytes 983048 | tf_op jit(solution)/shard_map/ppermute | solution.py:165
  69.5 60.0 %collective-permute-start.2 = (bf16[5,2,128,128]{3,2,1,0:T(8,128)(2,1)}, bf16[5,2,128,128]{3,2,1,0:T(8,128)(2,1)}, u32[]{:S(2)}, u32[]{:S(2)}) collective-permute-start(bf16[5,2,128,128]{3,2,1,0:T(8,128)(2,1)} %get-tuple-element.272), channel_id=1, source_target_pairs={{0,8},{4,12},{8,16},{12,20},{16,24},{20,28},{24,0},{28,4},{1,9},{5... | collective-permute-start | bytes 983048 | tf_op jit(solution)/shard_map/ppermute | solution.py:165
  76.3 57.9 %collective-permute-start.3 = (bf16[5,2,128,128]{3,2,1,0:T(8,128)(2,1)}, bf16[5,2,128,128]{3,2,1,0:T(8,128)(2,1)}, u32[]{:S(2)}, u32[]{:S(2)}) collective-permute-start(bf16[5,2,128,128]{3,2,1,0:T(8,128)(2,1)} %get-tuple-element.271), channel_id=1, source_target_pairs={{0,12},{4,16},{8,20},{12,24},{16,28},{20,0},{24,4},{28,8},{1,13},{... | collective-permute-start | bytes 983048 | tf_op jit(solution)/shard_map/ppermute | solution.py:165
  82.6 55.4 %collective-permute-start.4 = (bf16[5,2,128,128]{3,2,1,0:T(8,128)(2,1)}, bf16[5,2,128,128]{3,2,1,0:T(8,128)(2,1)}, u32[]{:S(2)}, u32[]{:S(2)}) collective-permute-start(bf16[5,2,128,128]{3,2,1,0:T(8,128)(2,1)} %get-tuple-element.270), channel_id=1, source_target_pairs={{0,16},{4,20},{8,24},{12,28},{16,0},{20,4},{24,8},{28,12},{1,17},{... | collective-permute-start | bytes 983048 | tf_op jit(solution)/shard_map/ppermute | solution.py:165
  82.6 57.8 %collective-permute-start.5 = (bf16[5,2,128,128]{3,2,1,0:T(8,128)(2,1)}, bf16[5,2,128,128]{3,2,1,0:T(8,128)(2,1)}, u32[]{:S(2)}, u32[]{:S(2)}) collective-permute-start(bf16[5,2,128,128]{3,2,1,0:T(8,128)(2,1)} %get-tuple-element.269), channel_id=1, source_target_pairs={{0,20},{4,24},{8,28},{12,0},{16,4},{20,8},{24,12},{28,16},{1,21},{... | collective-permute-start | bytes 983048 | tf_op jit(solution)/shard_map/ppermute | solution.py:165
  134.2 71.1 %collective-permute-start = (bf16[2,1024,128]{2,1,0:T(8,128)(2,1)S(1)}, bf16[2,1024,128]{2,1,0:T(8,128)(2,1)S(1)}, u32[]{:S(2)}, u32[]{:S(2)}) collective-permute-start(bf16[2,1024,128]{2,1,0:T(8,128)(2,1)S(1)} %get-tuple-element.210.own_ref), channel_id=1, source_target_pairs={{0,4},{4,8},{8,12},{12,16},{16,20},{20,24},{24,28},{1,5},{5,9},{9,... | collective-permute-start | bytes 1572872 | tf_op jit(solution)/shard_map/ppermute | solution.py:163
  154.2 46.5 %collective-permute-start.12 = (bf16[5,2,128,128]{3,2,1,0:T(8,128)(2,1)S(1)}, bf16[5,2,128,128]{3,2,1,0:T(8,128)(2,1)S(1)}, u32[]{:S(2)}, u32[]{:S(2)}) collective-permute-start(bf16[5,2,128,128]{3,2,1,0:T(8,128)(2,1)S(1)} %copy-done.22), channel_id=1, source_target_pairs={{0,16},{4,20},{8,24},{12,28},{16,0},{20,4},{24,8},{28,12},{1,17},{... | collective-permute-start | bytes 983048 | tf_op jit(solution)/shard_map/ppermute | solution.py:165
  232.0 173.2 %collective-permute-start.64 = (bf16[2,1024,128]{2,1,0:T(8,128)(2,1)S(1)}, bf16[2,1024,128]{2,1,0:T(8,128)(2,1)S(1)}, u32[]{:S(2)}, u32[]{:S(2)}) collective-permute-start(bf16[2,1024,128]{2,1,0:T(8,128)(2,1)S(1)} %get-tuple-element.85), channel_id=1, source_target_pairs={{4,0},{8,4},{12,8},{16,12},{20,16},{24,20},{28,24},{5,1},{9,5},{13... | collective-permute-start | bytes 1572872 | tf_op jit(solution)/shard_map/ppermute | solution.py:173
  241.8 48.5 %collective-permute-start.20 = (bf16[5,2,128,128]{3,2,1,0:T(8,128)(2,1)S(1)}, bf16[5,2,128,128]{3,2,1,0:T(8,128)(2,1)S(1)}, u32[]{:S(2)}, u32[]{:S(2)}) collective-permute-start(bf16[5,2,128,128]{3,2,1,0:T(8,128)(2,1)S(1)} %get-tuple-element.255), channel_id=1, source_target_pairs={{0,16},{4,20},{8,24},{12,28},{16,0},{20,4},{24,8},{28,12},{1,17},{... | collective-permute-start | bytes 983048 | tf_op jit(solution)/shard_map/ppermute | solution.py:165
  259.3 49.7 %collective-permute-start.22 = (bf16[5,2,128,128]{3,2,1,0:T(8,128)(2,1)S(1)}, bf16[5,2,128,128]{3,2,1,0:T(8,128)(2,1)S(1)}, u32[]{:S(2)}, u32[]{:S(2)}) collective-permute-start(bf16[5,2,128,128]{3,2,1,0:T(8,128)(2,1)S(1)} %get-tuple-element.253), channel_id=1, source_target_pairs={{0,24},{4,28},{8,0},{12,4},{16,8},{20,12},{24,16},{28,20},{1,25},{... | collective-permute-start | bytes 983048 | tf_op jit(solution)/shard_map/ppermute | solution.py:165
  260.9 52.2 %collective-permute-start.23 = (bf16[5,2,128,128]{3,2,1,0:T(8,128)(2,1)S(1)}, bf16[5,2,128,128]{3,2,1,0:T(8,128)(2,1)S(1)}, u32[]{:S(2)}, u32[]{:S(2)}) collective-permute-start(bf16[5,2,128,128]{3,2,1,0:T(8,128)(2,1)S(1)} %get-tuple-element.252), channel_id=1, source_target_pairs={{0,28},{4,0},{8,4},{12,8},{16,12},{20,16},{24,20},{28,24},{1,29},{... | collective-permute-start | bytes 983048 | tf_op jit(solution)/shard_map/ppermute | solution.py:165
  290.3 80.7 %collective-permute-start.16 = (bf16[2,1024,128]{2,1,0:T(8,128)(2,1)S(1)}, bf16[2,1024,128]{2,1,0:T(8,128)(2,1)S(1)}, u32[]{:S(2)}, u32[]{:S(2)}) collective-permute-start(bf16[2,1024,128]{2,1,0:T(8,128)(2,1)S(1)} %copy-done.18), channel_id=1, source_target_pairs={{0,4},{4,8},{8,12},{12,16},{16,20},{20,24},{24,28},{1,5},{5,9},{9,... | collective-permute-start | bytes 1572872 | tf_op jit(solution)/shard_map/ppermute | solution.py:163
  292.3 48.9 %collective-permute-start.25 = (bf16[5,2,128,128]{3,2,1,0:T(8,128)(2,1)S(1)}, bf16[5,2,128,128]{3,2,1,0:T(8,128)(2,1)S(1)}, u32[]{:S(2)}, u32[]{:S(2)}) collective-permute-start(bf16[5,2,128,128]{3,2,1,0:T(8,128)(2,1)S(1)} %get-tuple-element.251), channel_id=1, source_target_pairs={{0,4},{4,8},{8,12},{12,16},{16,20},{20,24},{24,28},{28,0},{1,5},{5... | collective-permute-start | bytes 983048 | tf_op jit(solution)/shard_map/ppermute | solution.py:165
  361.5 44.4 %collective-permute-start.65 = (bf16[2,1024,128]{2,1,0:T(8,128)(2,1)S(1)}, bf16[2,1024,128]{2,1,0:T(8,128)(2,1)S(1)}, u32[]{:S(2)}, u32[]{:S(2)}) collective-permute-start(bf16[2,1024,128]{2,1,0:T(8,128)(2,1)S(1)} %get-tuple-element.155), channel_id=1, source_target_pairs={{4,0},{8,4},{12,8},{16,12},{20,16},{24,20},{28,24},{5,1},{9,5},{13... | collective-permute-start | bytes 1572872 | tf_op jit(solution)/shard_map/ppermute | solution.py:173
  384.5 169.2 %collective-permute-start.66 = (bf16[2,1024,128]{2,1,0:T(8,128)(2,1)S(1)}, bf16[2,1024,128]{2,1,0:T(8,128)(2,1)S(1)}, u32[]{:S(2)}, u32[]{:S(2)}) collective-permute-start(bf16[2,1024,128]{2,1,0:T(8,128)(2,1)S(1)} %get-tuple-element.145), channel_id=1, source_target_pairs={{4,0},{8,4},{12,8},{16,12},{20,16},{24,20},{28,24},{5,1},{9,5},{13... | collective-permute-start | bytes 1572872 | tf_op jit(solution)/shard_map/ppermute | solution.py:173
  447.4 87.4 %collective-permute-start.32 = (bf16[2,1024,128]{2,1,0:T(8,128)(2,1)S(1)}, bf16[2,1024,128]{2,1,0:T(8,128)(2,1)S(1)}, u32[]{:S(2)}, u32[]{:S(2)}) collective-permute-start(bf16[2,1024,128]{2,1,0:T(8,128)(2,1)S(1)} %copy-done.16), channel_id=1, source_target_pairs={{0,4},{4,8},{8,12},{12,16},{16,20},{20,24},{24,28},{1,5},{5,9},{9,... | collective-permute-start | bytes 1572872 | tf_op jit(solution)/shard_map/ppermute | solution.py:163
  449.4 51.3 %collective-permute-start.41 = (bf16[5,2,128,128]{3,2,1,0:T(8,128)(2,1)S(1)}, bf16[5,2,128,128]{3,2,1,0:T(8,128)(2,1)S(1)}, u32[]{:S(2)}, u32[]{:S(2)}) collective-permute-start(bf16[5,2,128,128]{3,2,1,0:T(8,128)(2,1)S(1)} %get-tuple-element.237), channel_id=1, source_target_pairs={{0,4},{4,8},{8,12},{12,16},{16,20},{20,24},{24,28},{28,0},{1,5},{5... | collective-permute-start | bytes 983048 | tf_op jit(solution)/shard_map/ppermute | solution.py:165
  535.1 57.4 %collective-permute-start.49 = (bf16[5,2,128,128]{3,2,1,0:T(8,128)(2,1)S(1)}, bf16[5,2,128,128]{3,2,1,0:T(8,128)(2,1)S(1)}, u32[]{:S(2)}, u32[]{:S(2)}) collective-permute-start(bf16[5,2,128,128]{3,2,1,0:T(8,128)(2,1)S(1)} %get-tuple-element.230), channel_id=1, source_target_pairs={{0,4},{4,8},{8,12},{12,16},{16,20},{20,24},{24,28},{28,0},{1,5},{5... | collective-permute-start | bytes 983048 | tf_op jit(solution)/shard_map/ppermute | solution.py:165
  535.1 57.4 %collective-permute-start.50 = (bf16[5,2,128,128]{3,2,1,0:T(8,128)(2,1)S(1)}, bf16[5,2,128,128]{3,2,1,0:T(8,128)(2,1)S(1)}, u32[]{:S(2)}, u32[]{:S(2)}) collective-permute-start(bf16[5,2,128,128]{3,2,1,0:T(8,128)(2,1)S(1)} %get-tuple-element.229), channel_id=1, source_target_pairs={{0,8},{4,12},{8,16},{12,20},{16,24},{20,28},{24,0},{28,4},{1,9},{5... | collective-permute-start | bytes 983048 | tf_op jit(solution)/shard_map/ppermute | solution.py:165
  553.7 44.9 %collective-permute-start.52 = (bf16[5,2,128,128]{3,2,1,0:T(8,128)(2,1)S(1)}, bf16[5,2,128,128]{3,2,1,0:T(8,128)(2,1)S(1)}, u32[]{:S(2)}, u32[]{:S(2)}) collective-permute-start(bf16[5,2,128,128]{3,2,1,0:T(8,128)(2,1)S(1)} %get-tuple-element.227), channel_id=1, source_target_pairs={{0,16},{4,20},{8,24},{12,28},{16,0},{20,4},{24,8},{28,12},{1,17},{... | collective-permute-start | bytes 983048 | tf_op jit(solution)/shard_map/ppermute | solution.py:165
  596.1 75.4 %collective-permute-start.48 = (bf16[2,1024,128]{2,1,0:T(8,128)(2,1)S(1)}, bf16[2,1024,128]{2,1,0:T(8,128)(2,1)S(1)}, u32[]{:S(2)}, u32[]{:S(2)}) collective-permute-start(bf16[2,1024,128]{2,1,0:T(8,128)(2,1)S(1)} %copy-done.14), channel_id=1, source_target_pairs={{0,4},{4,8},{8,12},{12,16},{16,20},{20,24},{24,28},{1,5},{5,9},{9,... | collective-permute-start | bytes 1572872 | tf_op jit(solution)/shard_map/ppermute | solution.py:163
  630.5 56.5 %collective-permute-start.56 = (bf16[2,1024,128]{2,1,0:T(8,128)(2,1)S(1)}, bf16[2,1024,128]{2,1,0:T(8,128)(2,1)S(1)}, u32[]{:S(2)}, u32[]{:S(2)}) collective-permute-start(bf16[2,1024,128]{2,1,0:T(8,128)(2,1)S(1)} %copy-done.13), channel_id=1, source_target_pairs={{0,4},{4,8},{8,12},{12,16},{16,20},{20,24},{24,28},{1,5},{5,9},{9,... | collective-permute-start | bytes 1572872 | tf_op jit(solution)/shard_map/ppermute | solution.py:163
  658.3 51.3 %collective-permute-start.68 = (bf16[2,1024,128]{2,1,0:T(8,128)(2,1)S(1)}, bf16[2,1024,128]{2,1,0:T(8,128)(2,1)S(1)}, u32[]{:S(2)}, u32[]{:S(2)}) collective-permute-start(bf16[2,1024,128]{2,1,0:T(8,128)(2,1)S(1)} %get-tuple-element.135), channel_id=1, source_target_pairs={{4,0},{8,4},{12,8},{16,12},{20,16},{24,20},{28,24},{5,1},{9,5},{13... | collective-permute-start | bytes 1572872 | tf_op jit(solution)/shard_map/ppermute | solution.py:173
  660.3 49.3 %collective-permute-start.69 = (bf16[2,1024,128]{2,1,0:T(8,128)(2,1)S(1)}, bf16[2,1024,128]{2,1,0:T(8,128)(2,1)S(1)}, u32[]{:S(2)}, u32[]{:S(2)}) collective-permute-start(bf16[2,1024,128]{2,1,0:T(8,128)(2,1)S(1)} %get-tuple-element.175), channel_id=1, source_target_pairs={{4,0},{8,4},{12,8},{16,12},{20,16},{24,20},{28,24},{5,1},{9,5},{13... | collective-permute-start | bytes 1572872 | tf_op jit(solution)/shard_map/ppermute | solution.py:173
  (88 other events, 2460.4 us)

commit v2 on v1

v2 whole, which is shorter than its diff:
```python
import functools
import math

import jax
import jax.numpy as jnp
from jax import lax
from jax.experimental import pallas as pl
from jax.experimental.pallas import tpu as pltpu
from jax.sharding import PartitionSpec as P

WINDOW = 1024
BLOCK = 128
TOPK = 4
COLUMNS = 2
ROWS = 4
MASKED = -1e30
LAG = 2
FAR = 256
NT = (((1,), (1,)), ((), ()))
TN = (((0,), (0,)), ((), ()))
LOG2E = 1.4426950408889634
VM = pl.BlockSpec(memory_space=pltpu.VMEM)
SM = pl.BlockSpec(memory_space=pltpu.SMEM)
ANY = pl.BlockSpec(memory_space=pl.ANY)


def dot(a, b, dims=(((1,), (0,)), ((), ()))):
    return lax.dot_general(a, b, dims, preferred_element_type=jnp.float32)


def route_kernel(cap, per, list_ref, rank_ref, pick_ref, pack_ref, final_ref, count_ref, need_ref, seen, lines):
    owners = ROWS * COLUMNS
    row_len = TOPK + 1
    blocks = list_ref.shape[1] // row_len
    me = rank_ref[0]
    my_row, my_col = me // COLUMNS, me % COLUMNS
    for ref in (pick_ref, pack_ref, final_ref):
        for i in range(ref.shape[0]):
            ref[i] = 0
    need_ref[0] = 0

    def reader_block(step, carry):
        reader, block = lax.div(step, blocks), lax.rem(step, blocks)
        to_row, to_col = lax.div(reader, COLUMNS), lax.rem(reader, COLUMNS)
        place = reader ^ me

        @pl.when(block == 0)
        def _():
            for o in range(owners):
                seen[o] = 0
            for r in range(ROWS):
                lines[r] = 0

        used = list_ref[place, block * row_len + TOPK]

        @pl.when(reader == me)
        def _():
            count_ref[block] = used

        for s in range(TOPK):

            @pl.when(s < used)
            def _():
                entry = list_ref[place, block * row_len + s]
                owner = lax.div(entry, per)
                inside = entry - owner * per
                order = seen[owner]
                seen[owner] = order + 1
                row, col = lax.div(owner, COLUMNS), lax.rem(owner, COLUMNS)
                moved = (col != to_col).astype(jnp.int32)
                distance = row ^ to_row
                spot = lines[row]
                lines[row] = spot + 1

                @pl.when(distance > 0)
                def _():
                    need_ref[0] = jnp.maximum(need_ref[0], spot + 1)

                @pl.when(owner == me)
                def _():
                    pick_ref[(moved * ROWS + distance) * cap + order] = inside

                @pl.when((distance > 0) & (row == my_row) & (to_col == my_col))
                def _():
                    pack_ref[(distance - 1) * 2 * cap + spot] = (moved * (ROWS - 1) + distance - 1) * cap + order

                @pl.when(reader == me)
                def _():
                    final_ref[block * TOPK + s] = jnp.where(distance == 0, moved * cap + order, distance * FAR + spot)

        return carry

    lax.fori_loop(0, owners * blocks, reader_block, 0)


def route(lists, rank, cap, per):
    owners, width = lists.shape
    blocks = width // (TOPK + 1)
    i32 = lambda n: jax.ShapeDtypeStruct((n,), jnp.int32)
    return pl.pallas_call(
        functools.partial(route_kernel, cap, per),
        out_shape=(i32(2 * ROWS * cap), i32(2 * (ROWS - 1) * cap), i32(blocks * TOPK), i32(blocks), i32(1)),
        in_specs=[SM, SM],
        out_specs=[SM] * 5,
        scratch_shapes=[pltpu.SMEM((owners,), jnp.int32), pltpu.SMEM((ROWS,), jnp.int32)],
        name="route",
    )(lists, rank)


def pick_kernel(table_ref, key_ref, value_ref, *outs):
    first = 0
    for out in outs:

        def place(i, carry, out=out, first=first):
            at = table_ref[first + i]
            out[i, 0] = key_ref[at]
            out[i, 1] = value_ref[at]
            return carry

        lax.fori_loop(0, out.shape[0], place, 0)
        first += out.shape[0]


def pick(head, table, keys, values):
    head_dim = keys.shape[-1]
    whole = pl.BlockSpec((None,) + keys.shape[1:], lambda i: (head, 0, 0, 0))
    size = table.shape[0] // 2
    return pl.pallas_call(
        pick_kernel,
        grid=(1,),
        out_shape=[jax.ShapeDtypeStruct((size, 2, BLOCK, head_dim), keys.dtype)] * 2,
        in_specs=[SM, whole, whole],
        out_specs=[pl.BlockSpec((size, 2, BLOCK, head_dim), lambda i: (0, 0, 0, 0))] * 2,
        compiler_params=pltpu.CompilerParams(vmem_limit_bytes=32 << 20),
        cost_estimate=pl.CostEstimate(flops=0, bytes_accessed=1 << 16, transcendentals=0),
        name="pick",
    )(table, keys, values)


def pack_kernel(cap, table_ref, stay_ref, side_ref, *rest):
    *outs, held, sem = rest
    size = (ROWS - 1) * cap
    moves = [
        pltpu.make_async_copy(ref.at[cap:], held.at[i * size : (i + 1) * size], sem.at[i])
        for i, ref in enumerate((stay_ref, side_ref))
    ]
    for move in moves:
        move.start()
    for move in moves:
        move.wait()
    for d, out in enumerate(outs):

        def place(i, carry, d=d, out=out):
            out[i] = held[table_ref[d * 2 * cap + i]]
            return carry

        lax.fori_loop(0, out.shape[0], place, 0)


def pack(cap, length, table, stay, side):
    block = stay.shape[1:]
    return pl.pallas_call(
        functools.partial(pack_kernel, cap),
        out_shape=[jax.ShapeDtypeStruct((length,) + block, stay.dtype)] * (ROWS - 1),
        in_specs=[SM, ANY, ANY],
        out_specs=[VM] * (ROWS - 1),
        scratch_shapes=[
            pltpu.VMEM((2 * (ROWS - 1) * cap,) + block, stay.dtype), pltpu.SemaphoreType.DMA((2,))
        ],
        compiler_params=pltpu.CompilerParams(vmem_limit_bytes=16 << 20),
        cost_estimate=pl.CostEstimate(flops=0, bytes_accessed=1 << 16, transcendentals=0),
        name="pack",
    )(table, stay, side)


def attention_kernel(
    cap, final_ref, count_ref, first_ref, qg_ref, prev_ref, own_ref, *rest
):
    *sources, o_ref, dq_ref, stat_ref, dk_ref, dv_ref, mem, kx, vx, dkx, dvx, sem = rest
    tokens, head_dim = qg_ref.shape[1:]
    span = WINDOW + BLOCK
    scale = 1.0 / math.sqrt(head_dim)
    moves, at = [], 0
    for i, ref in enumerate(sources):
        size = cap if i < 2 else ref.shape[0]
        moves.append(pltpu.make_async_copy(ref.at[:size], mem.at[at : at + size], sem.at[i]))
        moves[i].start()
        at += size
    far_size = sources[-1].shape[0]
    kx[:WINDOW] = prev_ref[0]
    kx[WINDOW:] = own_ref[0]
    vx[:WINDOW] = prev_ref[1]
    vx[WINDOW:] = own_ref[1]
    dkx[...] = jnp.zeros_like(dkx)
    dvx[...] = jnp.zeros_like(dvx)
    for move in moves:
        move.wait()
    start_col = first_ref[0] * WINDOW
    row = lax.broadcasted_iota(jnp.int32, (BLOCK, span), 0)
    col = lax.broadcasted_iota(jnp.int32, (BLOCK, span), 1)
    gap = col - row
    lane = lax.broadcasted_iota(jnp.int32, (BLOCK, BLOCK), 1)

    def block_step(b, carry):
        r0 = pl.multiple_of(b * BLOCK, BLOCK)
        rows = pl.ds(r0, BLOCK)
        window = pl.ds(r0, span)
        q = qg_ref[0, rows, :]
        g = qg_ref[1, rows, :]
        kw = kx[window, :]
        vw = vx[window, :]
        seen = (gap > 0) & (gap <= WINDOW) & (col >= start_col - r0)
        s = jnp.where(seen, dot(q, kw, NT) * (scale * LOG2E), MASKED)
        used = count_ref[b]
        km, vm, sm = [], [], []
        top = jnp.max(s, 1, keepdims=True)
        for i in range(TOPK):
            code = final_ref[b * TOPK + i]
            line, slot = code // FAR, code % FAR
            slot = jnp.where(line == 0, slot, 2 * cap + (line - 1) * far_size + slot)
            km.append(mem[slot, 0])
            vm.append(mem[slot, 1])
            far = dot(q, km[i], NT) * (scale * LOG2E)
            sm.append(jnp.where(i < used, far, MASKED))
            top = jnp.maximum(top, jnp.max(sm[i], 1, keepdims=True))
        p = jnp.exp2(s - top)
        total = jnp.sum(p, 1, keepdims=True)
        pm = []
        for i in range(TOPK):
            pm.append(jnp.exp2(sm[i] - top))
            total = total + jnp.sum(pm[i], 1, keepdims=True)
        inv = 1.0 / total
        p = p * inv
        pb = p.astype(jnp.bfloat16)
        o = dot(pb, vw)
        for i in range(TOPK):
            pm[i] = pm[i] * inv
            o = o + dot(pm[i].astype(jnp.bfloat16), vm[i])
        o = o.astype(jnp.bfloat16)
        o_ref[rows, :] = o
        delta = jnp.sum(g.astype(jnp.float32) * o.astype(jnp.float32), 1, keepdims=True)
        ds = (p * (dot(g, vw, NT) - delta)).astype(jnp.bfloat16)
        dq = dot(ds, kw)
        for i in range(TOPK):
            dsm = (pm[i] * (dot(g, vm[i], NT) - delta)).astype(jnp.bfloat16)
            dq = dq + dot(dsm, km[i])
        dq_ref[rows, :] = (dq * scale).astype(jnp.bfloat16)
        both = jnp.where(lane < BLOCK // 2, top + jnp.log2(total), delta).T
        stat_ref[0:1, rows] = both[0:1]
        stat_ref[1:2, rows] = both[BLOCK // 2 : BLOCK // 2 + 1]
        dkx[window, :] += dot(ds, q, TN)
        dvx[window, :] += dot(pb, g, TN)
        return carry

    lax.fori_loop(0, tokens // BLOCK, block_step, 0)
    dk_ref[...] = dkx[WINDOW:]
    dv_ref[...] = dvx[WINDOW:]


def of_head(head, a):
    return pl.BlockSpec((a.shape[0], None) + a.shape[2:], lambda i: (0, head, 0, 0))


def attend(cap, final, counts, first, head, qg, at, prev, own, *sources):
    tokens, head_dim = qg.shape[2:]
    ext = tokens + WINDOW
    slots = 2 * cap + sum(s.shape[0] for s in sources[2:])
    row16 = jax.ShapeDtypeStruct((tokens, head_dim), jnp.bfloat16)
    row32 = jax.ShapeDtypeStruct((tokens, head_dim), jnp.float32)
    return pl.pallas_call(
        functools.partial(attention_kernel, cap),
        out_shape=(row16, row16, jax.ShapeDtypeStruct((2, tokens), jnp.float32), row32, row32),
        grid=(1,),
        in_specs=[SM] * 3 + [of_head(head, qg), of_head(at, prev), of_head(head, own)] + [ANY] * len(sources),
        out_specs=[VM] * 5,
        scratch_shapes=[
            pltpu.VMEM((slots, 2, BLOCK, head_dim), jnp.bfloat16),
            pltpu.VMEM((ext, head_dim), jnp.bfloat16),
            pltpu.VMEM((ext, head_dim), jnp.bfloat16),
            pltpu.VMEM((ext, head_dim), jnp.float32),
            pltpu.VMEM((ext, head_dim), jnp.float32),
            pltpu.SemaphoreType.DMA((len(sources),)),
        ],
        compiler_params=pltpu.CompilerParams(vmem_limit_bytes=32 << 20),
        cost_estimate=pl.CostEstimate(flops=128 * tokens * tokens * head_dim, bytes_accessed=1 << 16, transcendentals=0),
        name="attend",
    )(final, counts, first, qg, prev, own, *sources)


def back_kernel(stat_ref, next_ref, own_ref, dk_in, dv_in, dk_ref, dv_ref):
    tokens, head_dim = dk_in.shape
    scale = 1.0 / math.sqrt(head_dim)
    size = 2 * BLOCK
    for j in range(tokens // size):
        rows = slice(j * size, (j + 1) * size)
        seen = (j + 1) * size
        k, v = own_ref[0, rows], own_ref[1, rows]
        q, g = next_ref[0, :seen], next_ref[1, :seen]
        key = lax.broadcasted_iota(jnp.int32, (size, seen), 0) + j * size
        query = lax.broadcasted_iota(jnp.int32, (size, seen), 1)
        s = dot(k, q, NT) * (scale * LOG2E) - stat_ref[0:1, :seen]
        p = jnp.exp2(jnp.where(key > query, s, MASKED))
        ds = (p * (dot(v, g, NT) - stat_ref[1:2, :seen])).astype(jnp.bfloat16)
        dk_ref[rows] = ((dk_in[rows] + dot(ds, q)) * scale).astype(jnp.bfloat16)
        dv_ref[rows] = (dv_in[rows] + dot(p.astype(jnp.bfloat16), g)).astype(jnp.bfloat16)


def add_back(head, stat, at, following, own, dk, dv):
    tokens, head_dim = dk.shape
    row16 = jax.ShapeDtypeStruct((tokens, head_dim), jnp.bfloat16)
    return pl.pallas_call(
        back_kernel,
        out_shape=(row16, row16),
        grid=(1,),
        in_specs=[VM, of_head(at, following), of_head(head, own), VM, VM],
        out_specs=[VM] * 2,
        compiler_params=pltpu.CompilerParams(vmem_limit_bytes=32 << 20),
        cost_estimate=pl.CostEstimate(flops=0, bytes_accessed=1 << 16, transcendentals=0),
        name="add_back",
    )(stat, following, own, dk, dv)


def after(x, *earlier):
    earlier = [e for e in earlier if e is not None]
    return lax.optimization_barrier((x, *earlier))[0] if earlier else x


def shards(queries, seg_keys, seg_values, mem_keys, mem_values, mem_blocks, mem_count, grad_out):
    tokens, heads, head_dim = queries.shape
    owners = lax.axis_size("seq")
    rank = lax.axis_index("seq")
    n_blocks = tokens // BLOCK
    per = mem_keys.shape[0] // BLOCK
    live_total = n_blocks * (TOPK + 1) // 2
    cap = max(2, 2 * live_total // owners)
    along = [(i, i + 1) for i in range(owners - 1)]
    back = [(i + 1, i) for i in range(owners - 1)]
    shift = lambda d: [(i, (i + d) % owners) for i in range(owners)]

    lists = jnp.concatenate([mem_blocks, mem_count[:, None]], 1)
    lists = lax.all_gather(lists, "head", axis=0, tiled=True).reshape(1, -1)
    while lists.shape[0] < owners:
        size = lists.shape[0]
        with jax.named_scope(f"lists{size}"):
            theirs = lax.ppermute(lists, "seq", [(i, i ^ size) for i in range(owners)])
        lists = jnp.concatenate([lists, theirs], 0)

    first = (rank == 0).astype(jnp.int32)[None]
    major = lambda a: jnp.moveaxis(a, 1, 0)
    kv = jnp.stack([major(seg_keys), major(seg_values)], 0)
    qg = jnp.stack([major(queries), major(grad_out)], 0)

    held_keys, held_values = after((mem_keys, mem_values), lists)
    keys, values = (
        jnp.moveaxis(m.reshape(per, BLOCK, heads, head_dim), 2, 0) for m in (held_keys, held_values)
    )

    def border(cut, *earlier):
        up, down = after((kv[:, cut], qg[:, cut]), *earlier)
        with jax.named_scope(f"prev_kv{cut.start}"):
            up = lax.ppermute(up, "seq", along)
        with jax.named_scope(f"next_qg{cut.start}"):
            down = lax.ppermute(down, "seq", back)
        return up, down

    def in_rows(outs):
        return tuple(jnp.stack([o[i] for o in outs], 1) for i in range(4))

    def finish(head, final, counts, borders, *sources):
        prev_kv, next_qg, at = borders[head]
        o, dq, stat, dk, dv = attend(
            cap, final, counts, first, head, qg, at, prev_kv, kv, *sources
        )
        with jax.named_scope(f"stat{head}"):
            stat = lax.ppermute(stat, "seq", back)
        dk, dv = add_back(head, stat, at, next_qg, kv, dk, dv)
        return o, dq, dk, dv

    def direct():
        packed = lists[jnp.arange(owners) ^ rank].reshape(owners, n_blocks, TOPK + 1)
        ids = packed[:, :, :TOPK].reshape(owners, n_blocks * TOPK)
        counts = packed[:, :, TOPK]
        live = (jnp.arange(TOPK, dtype=jnp.int32) < counts[:, :, None]).reshape(owners, -1)
        owner_of = ids // per
        one_hot = (owner_of[:, :, None] == jnp.arange(owners, dtype=jnp.int32)) & live[:, :, None]
        order = jnp.sum((jnp.cumsum(one_hot.astype(jnp.int32), 1) - 1) * one_hot, 2)
        asked = (owner_of == rank) & live
        chosen = asked[:, :, None] & (order[:, :, None] == jnp.arange(cap, dtype=jnp.int32))
        send_idx = jnp.roll(jnp.sum(jnp.where(chosen, (ids % per)[:, :, None], 0), 1), -rank, 0)
        final = jnp.where(live, ((rank - owner_of) % owners) * cap + order, 0)
        final = lax.dynamic_index_in_dim(final, rank, 0, keepdims=False)
        counts = lax.dynamic_index_in_dim(counts, rank, 0, keepdims=False)
        borders = [border(slice(h, h + 1)) + (0,) for h in range(heads)]
        arrived = []
        for h in range(heads):
            send = jnp.stack([keys[h][send_idx], values[h][send_idx]], 2)
            if h >= 2:
                send = after(send, *arrived[h - 2])
            arrived.append([send[0]] + [lax.ppermute(send[d], "seq", shift(d)) for d in range(1, owners)])
        return in_rows([finish(h, final, counts, borders, *arrived[h]) for h in range(heads)])

    if owners != ROWS * COLUMNS:
        return direct()

    pick_table, pack_table, final, counts, need = route(lists, rank[None], cap, per)
    early = min(2, heads)
    first_border = border(slice(0, early), lists)

    def by_rows(length):
        picked = [pick(h, pick_table, keys, values) for h in range(heads)]
        swap = [(i, i ^ 1) for i in range(owners)]
        with jax.named_scope("side0"):
            side = [lax.ppermute(picked[0][1], "seq", swap)]
        borders = [first_border + (h,) for h in range(early)]
        lines, outs = [], []

        def complete(h):
            ready = after(counts, lines[h + 1][2]) if h + 1 < heads else counts
            outs.append(finish(h, final, ready, borders, picked[h][0], side[h], *lines[h]))

        earlier = list(first_border)
        for h in range(heads):
            sends = list(pack(cap, length, pack_table, picked[h][0], side[h]))
            if h + 1 < heads:
                sends.append(picked[h + 1][1])
            if h + early < heads:
                cut = slice(h + early, h + early + 1)
                sends += [kv[:, cut], qg[:, cut]]
            sends = list(lax.optimization_barrier((sends, earlier))[0])
            sent = []
            for d in range(ROWS - 1):
                with jax.named_scope(f"lines{h}_{d}"):
                    route = [(i, i ^ (COLUMNS * (d + 1))) for i in range(owners)]
                    sent.append(lax.ppermute(sends[d], "seq", route))
            lines.append(sent)
            earlier = list(sent)
            if h + 1 < heads:
                with jax.named_scope(f"side{h + 1}"):
                    side.append(lax.ppermute(sends[3], "seq", swap))
                earlier.append(side[h + 1])
            if h + early < heads:
                with jax.named_scope(f"prev_kv{h + early}"):
                    up = lax.ppermute(sends[4], "seq", along)
                with jax.named_scope(f"next_qg{h + early}"):
                    down = lax.ppermute(sends[5], "seq", back)
                borders.append((up, down, 0))
                earlier += [up, down]
            if h >= 1:
                complete(h - 1)
                earlier.append(outs[h - 1][0])
            if h >= 2:
                earlier.append(outs[h - 2][2])
        complete(heads - 1)
        return in_rows(outs)

    longest = 2 * cap
    sizes = [longest - 2, longest - 1, longest]
    index = jnp.clip(need[0] - sizes[0], 0, 2)
    return lax.switch(index, [functools.partial(by_rows, n) for n in sizes])


def solution(mesh):
    rows = P("seq", "head", None)
    return jax.shard_map(
        shards,
        mesh=mesh,
        in_specs=(rows, rows, rows, rows, rows, P(("seq", "head"), None), P(("seq", "head")), rows),
        out_specs=(rows, rows, rows, rows),
        check_vma=False,
    )
```

time: 729 us -> 609 us (0.84)
  starting transfers between devices: 268 us -> 106 us
  Pallas kernels: 13.4 us -> 148 us
  other arithmetic: 111 us -> 9.78 us
  waiting for transfers between devices: 201 us -> 243 us
  blocking collectives: 31.4 us -> 5.06 us
  local copies, waits for them, and re-layouts: 89.4 us -> 73.2 us
  loops' own time: 0 us -> 9.56 us
    ppermute x72 -> x57, starting transfers between devices: 268 us -> 106 us  [the longest x8 27.1 us: finish(): stat = lax.ppermute(stat, 'seq', back)]
    pallas_call x1 -> x30, Pallas kernels: 13.4 us -> 148 us  [the longest x8 110 us: attend(): pl.pallas_call(functools.partial(attention_kernel, cap), out_shape=(row16...]
    pallas_call x7 -> x0, other arithmetic: 94.1 us -> none  [attend(): pl.pallas_call(attention_kernel, out_shape=(row16, row16, jax.ShapeDtypeS...]
    unnamed x150 -> x12, local copies, waits for them, and re-layouts: 44.9 us -> 0.03 us
    cond x0 -> x146, local copies, waits for them, and re-layouts: none -> 42 us
    ppermute x72 -> x57, waiting for transfers between devices: 201 us -> 243 us  [the longest x24 82.3 us: by_rows(): sent.append(lax.ppermute(sends[d], 'seq', route))]
    gather x8 -> x0, local copies, waits for them, and re-layouts: 31.4 us -> none  [shards(): send = mem_major[h][send_idx]]
    all_gather x1, blocking collectives: 31.4 us -> 5.06 us  [shards(): lists = lax.all_gather(lists, 'head', axis=0, tiled=True).reshape(1, -1)]
  transfers between devices with their start and end apart: 72 -> 57, of which waited for: 23 -> 29; matrix products, arithmetic and copies ran while one was open for 21% -> 9% of each run, Pallas kernels for 0% -> 24%
where the time goes in v2:
time: 609 us; the launch traced here: 597 us
  waiting for transfers between devices  243 us (40%)
  Pallas kernels  148 us (24%)
  starting transfers between devices  106 us (17%)
  local copies, waits for them, and re-layouts  73.2 us (12%)
  other arithmetic  9.78 us (2%)
  loops' own time  9.56 us (2%)
    pallas_call x8, Pallas kernels, attend(): pl.pallas_call(functools.partial(attention_kernel, cap), out_shape=(row16...  110 us
    ppermute x24, waiting for transfers between devices, by_rows(): sent.append(lax.ppermute(sends[d], 'seq', route))  82.3 us
    ppermute x7, waiting for transfers between devices, by_rows(): side.append(lax.ppermute(sends[3], 'seq', swap))  71.8 us
    ppermute x6, waiting for transfers between devices, by_rows(): up = lax.ppermute(sends[4], 'seq', along)  46 us
    cond x142, local copies, waits for them, and re-layouts  31.3 us
    ppermute x8, starting transfers between devices, finish(): stat = lax.ppermute(stat, 'seq', back)  27.1 us
    ppermute x24, starting transfers between devices, by_rows(): sent.append(lax.ppermute(sends[d], 'seq', route))  24.8 us
    ppermute x6, starting transfers between devices, by_rows(): up = lax.ppermute(sends[4], 'seq', along)  19.6 us
  transfers between devices with their start and end apart: 57, of which 29 were waited for; matrix products, arithmetic and copies ran while one was open for 9% of the time, Pallas kernels for 24%

profile of v2, /device:TPU:16, one launch (start us, length us, event | category | flops | bytes accessed | tf_op | source)
XLA Modules:
  0.0 597.2 jit_solution(1545272669592573961)
XLA Ops:
  35.3 8.7 %route.1 = (s32[40]{0:T(128)S(1)}, s32[30]{0:T(128)S(1)}, s32[32]{0:T(128)S(1)}, s32[8]{0:T(128)S(1)}, s32[1]{0:T(128)}) custom-call(s32[8,40]{1,0:T(8,128)} %pad_add_fusion.list_ref, s32[1]{0:T(128)} %bitcast.101.rank_ref), custom_call_target="tpu_custom_call" | custom-call | tf_op jit(solution)/shard_map/route/pallas_call | solution.py:100
  43.9 7.8 %copy.36 = bf16[4096,8,128]{2,0,1:T(8,128)(2,1)} copy(bf16[4096,8,128]{2,1,0:T(8,128)(2,1)} %param.14) | data formatting | bytes 16777216 | tf_op jit(solution)/shard_map/optimization_barrier | solution.py:325
  69.6 526.4 %conditional.1 = (bf16[1024,8,128]{2,1,0:T(8,128)(2,1)}, bf16[1024,8,128]{2,1,0:T(8,128)(2,1)}, bf16[1024,8,128]{2,1,0:T(8,128)(2,1)}, bf16[1024,8,128]{2,1,0:T(8,128)(2,1)}) conditional(s32[]{:T(128)} %bitcast.102, (s32[40]{0:T(128)S(1)}, bf16[8,32,128,128]{3,2,1,0:T(8,128)(2,1)}, bf16[8,32,128,128]{3,2,1,0:T(8,128)(2,1)}, ...), branch_computations={%region_0.1_spmd, %region_1.2_spmd, %region_2.3_spmd} | conditional | flops 137438953472 | bytes 519664352 | solution.py:459
  83.1 19.4 %collective-permute-done.side_ref.rest_1_ = bf16[20,2,128,128]{3,2,1,0:T(8,128)(2,1)S(1)} collective-permute-done((bf16[20,2,128,128]{3,2,1,0:T(8,128)(2,1)S(1)}, bf16[20,2,128,128]{3,2,1,0:T(8,128)(2,1)S(1)}, u32[]{:S(2)}, u32[]{:S(2)}) %collective-permute-start) | collective-permute-done | bytes 1310752 | tf_op jit(solution)/shard_map/cond/branch_0_fun/side0/ppermute | solution.py:413
  111.4 22.4 %collective-permute-done.1.side_ref.rest_1_ = bf16[20,2,128,128]{3,2,1,0:T(8,128)(2,1)S(1)} collective-permute-done((bf16[20,2,128,128]{3,2,1,0:T(8,128)(2,1)S(1)}, bf16[20,2,128,128]{3,2,1,0:T(8,128)(2,1)S(1)}, u32[]{:S(2)}, u32[]{:S(2)}) %collective-permute-start.1) | collective-permute-done | bytes 1310752 | tf_op jit(solution)/shard_map/cond/branch_0_fun/side1/ppermute | solution.py:439
  141.1 11.3 %collective-permute-done.4.rest_4_ = bf16[8,2,128,128]{3,2,1,0:T(8,128)(2,1)S(1)} collective-permute-done((bf16[8,2,128,128]{3,2,1,0:T(8,128)(2,1)S(1)}, bf16[8,2,128,128]{3,2,1,0:T(8,128)(2,1)S(1)}, u32[]{:S(2)}, u32[]{:S(2)}) %collective-permute-start.4) | collective-permute-done | bytes 524320 | tf_op jit(solution)/shard_map/cond/branch_0_fun/lines0_2/ppermute | solution.py:434
  152.3 23.6 %collective-permute-done.5.prev_ref = bf16[2,1,1024,128]{3,2,1,0:T(8,128)(2,1)S(1)} collective-permute-done((bf16[2,1,1024,128]{3,2,1,0:T(8,128)(2,1)S(1)}, bf16[2,1,1024,128]{3,2,1,0:T(8,128)(2,1)S(1)}, u32[]{:S(2)}, u32[]{:S(2)}) %collective-permute-start.5) | collective-permute-done | bytes 524320 | tf_op jit(solution)/shard_map/cond/branch_0_fun/prev_kv2/ppermute | solution.py:443
  204.4 14.5 %attend.24 = (bf16[1024,128]{1,0:T(8,128)(2,1)S(1)}, bf16[1024,128]{1,0:T(8,128)(2,1)S(1)}, f32[2,1024]{1,0:T(2,128)S(1)}, f32[1024,128]{1,0:T(8,128)S(1)}, f32[1024,128]{1,0:T(8,128)S(1)}) custom-call(s32[32]{0:T(128)S(1)} %get-tuple-element.66.final_ref, s32[8]{0:T(128)S(1)} %get-tuple-element.190.count_ref, s32[1]{0:T(128)} %bitcast.first_ref, ...), custom_call_target="tpu_custom_call" | custom-call | flops 17179869184 | bytes 65536 | tf_op jit(solution)/shard_map/cond/branch_0_fun/attend/pallas_call | solution.py:270
  219.6 11.9 %collective-permute-done.8.side_ref.rest_1_ = bf16[20,2,128,128]{3,2,1,0:T(8,128)(2,1)S(1)} collective-permute-done((bf16[20,2,128,128]{3,2,1,0:T(8,128)(2,1)}, bf16[20,2,128,128]{3,2,1,0:T(8,128)(2,1)S(1)}, u32[]{:S(2)}, u32[]{:S(2)}) %collective-permute-start.8) | collective-permute-done | bytes 1310752 | tf_op jit(solution)/shard_map/cond/branch_0_fun/side2/ppermute | solution.py:439
  250.8 18.5 %collective-permute-done.13.rest_4_ = bf16[8,2,128,128]{3,2,1,0:T(8,128)(2,1)S(1)} collective-permute-done((bf16[8,2,128,128]{3,2,1,0:T(8,128)(2,1)S(1)}, bf16[8,2,128,128]{3,2,1,0:T(8,128)(2,1)S(1)}, u32[]{:S(2)}, u32[]{:S(2)}) %collective-permute-start.13) | collective-permute-done | bytes 524320 | tf_op jit(solution)/shard_map/cond/branch_0_fun/lines2_2/ppermute | solution.py:434
  271.3 14.9 %attend.25 = (bf16[1024,128]{1,0:T(8,128)(2,1)S(1)}, bf16[1024,128]{1,0:T(8,128)(2,1)S(1)}, f32[2,1024]{1,0:T(2,128)S(1)}, f32[1024,128]{1,0:T(8,128)S(1)}, f32[1024,128]{1,0:T(8,128)S(1)}) custom-call(s32[32]{0:T(128)S(1)} %get-tuple-element.66.final_ref, s32[8]{0:T(128)S(1)} %get-tuple-element.190.count_ref, s32[1]{0:T(128)} %bitcast.first_ref, ...), custom_call_target="tpu_custom_call" | custom-call | flops 17179869184 | bytes 65536 | tf_op jit(solution)/shard_map/cond/branch_0_fun/attend/pallas_call | solution.py:270
  305.4 10.4 %collective-permute-done.20.rest_4_ = bf16[8,2,128,128]{3,2,1,0:T(8,128)(2,1)S(1)} collective-permute-done((bf16[8,2,128,128]{3,2,1,0:T(8,128)(2,1)S(1)}, bf16[8,2,128,128]{3,2,1,0:T(8,128)(2,1)S(1)}, u32[]{:S(2)}, u32[]{:S(2)}) %collective-permute-start.20) | collective-permute-done | bytes 524320 | tf_op jit(solution)/shard_map/cond/branch_0_fun/lines3_2/ppermute | solution.py:434
  317.8 13.5 %attend.26 = (bf16[1024,128]{1,0:T(8,128)(2,1)S(1)}, bf16[1024,128]{1,0:T(8,128)(2,1)S(1)}, f32[2,1024]{1,0:T(2,128)S(1)}, f32[1024,128]{1,0:T(8,128)S(1)}, f32[1024,128]{1,0:T(8,128)S(1)}) custom-call(s32[32]{0:T(128)S(1)} %get-tuple-element.66.final_ref, s32[8]{0:T(128)S(1)} %get-tuple-element.190.count_ref, s32[1]{0:T(128)} %bitcast.first_ref, ...), custom_call_target="tpu_custom_call" | custom-call | flops 17179869184 | bytes 65536 | tf_op jit(solution)/shard_map/cond/branch_0_fun/attend/pallas_call | solution.py:270
  332.0 10.1 %collective-permute-done.21.side_ref.rest_1_ = bf16[20,2,128,128]{3,2,1,0:T(8,128)(2,1)S(1)} collective-permute-done((bf16[20,2,128,128]{3,2,1,0:T(8,128)(2,1)S(1)}, bf16[20,2,128,128]{3,2,1,0:T(8,128)(2,1)S(1)}, u32[]{:S(2)}, u32[]{:S(2)}) %collective-permute-start.21) | collective-permute-done | bytes 1310752 | tf_op jit(solution)/shard_map/cond/branch_0_fun/side4/ppermute | solution.py:439
  345.5 10.1 %collective-permute-done.24.prev_ref = bf16[2,1,1024,128]{3,2,1,0:T(8,128)(2,1)S(1)} collective-permute-done((bf16[2,1,1024,128]{3,2,1,0:T(8,128)(2,1)S(1)}, bf16[2,1,1024,128]{3,2,1,0:T(8,128)(2,1)S(1)}, u32[]{:S(2)}, u32[]{:S(2)}) %collective-permute-start.24) | collective-permute-done | bytes 524320 | tf_op jit(solution)/shard_map/cond/branch_0_fun/prev_kv5/ppermute | solution.py:443
  372.5 13.5 %attend.27 = (bf16[1024,128]{1,0:T(8,128)(2,1)S(1)}, bf16[1024,128]{1,0:T(8,128)(2,1)S(1)}, f32[2,1024]{1,0:T(2,128)S(1)}, f32[1024,128]{1,0:T(8,128)S(1)}, f32[1024,128]{1,0:T(8,128)S(1)}) custom-call(s32[32]{0:T(128)S(1)} %get-tuple-element.66.final_ref, s32[8]{0:T(128)S(1)} %get-tuple-element.190.count_ref, s32[1]{0:T(128)} %bitcast.first_ref, ...), custom_call_target="tpu_custom_call" | custom-call | flops 17179869184 | bytes 65536 | tf_op jit(solution)/shard_map/cond/branch_0_fun/attend/pallas_call | solution.py:270
  386.7 13.2 %collective-permute-done.28.side_ref.rest_1_ = bf16[20,2,128,128]{3,2,1,0:T(8,128)(2,1)S(1)} collective-permute-done((bf16[20,2,128,128]{3,2,1,0:T(8,128)(2,1)S(1)}, bf16[20,2,128,128]{3,2,1,0:T(8,128)(2,1)S(1)}, u32[]{:S(2)}, u32[]{:S(2)}) %collective-permute-start.28) | collective-permute-done | bytes 1310752 | tf_op jit(solution)/shard_map/cond/branch_0_fun/side5/ppermute | solution.py:439
  423.2 9.3 %collective-permute-done.34.rest_4_ = bf16[8,2,128,128]{3,2,1,0:T(8,128)(2,1)S(1)} collective-permute-done((bf16[8,2,128,128]{3,2,1,0:T(8,128)(2,1)S(1)}, bf16[8,2,128,128]{3,2,1,0:T(8,128)(2,1)S(1)}, u32[]{:S(2)}, u32[]{:S(2)}) %collective-permute-start.34) | collective-permute-done | bytes 524320 | tf_op jit(solution)/shard_map/cond/branch_0_fun/lines5_2/ppermute | solution.py:434
  434.4 13.5 %attend.28 = (bf16[1024,128]{1,0:T(8,128)(2,1)S(1)}, bf16[1024,128]{1,0:T(8,128)(2,1)S(1)}, f32[2,1024]{1,0:T(2,128)S(1)}, f32[1024,128]{1,0:T(8,128)S(1)}, f32[1024,128]{1,0:T(8,128)S(1)}) custom-call(s32[32]{0:T(128)S(1)} %get-tuple-element.66.final_ref, s32[8]{0:T(128)S(1)} %get-tuple-element.190.count_ref, s32[1]{0:T(128)} %bitcast.first_ref, ...), custom_call_target="tpu_custom_call" | custom-call | flops 17179869184 | bytes 65536 | tf_op jit(solution)/shard_map/cond/branch_0_fun/attend/pallas_call | solution.py:270
  448.6 11.6 %collective-permute-done.35.side_ref.rest_1_ = bf16[20,2,128,128]{3,2,1,0:T(8,128)(2,1)S(1)} collective-permute-done((bf16[20,2,128,128]{3,2,1,0:T(8,128)(2,1)S(1)}, bf16[20,2,128,128]{3,2,1,0:T(8,128)(2,1)S(1)}, u32[]{:S(2)}, u32[]{:S(2)}) %collective-permute-start.35) | collective-permute-done | bytes 1310752 | tf_op jit(solution)/shard_map/cond/branch_0_fun/side6/ppermute | solution.py:439
  488.0 13.5 %attend.29 = (bf16[1024,128]{1,0:T(8,128)(2,1)S(1)}, bf16[1024,128]{1,0:T(8,128)(2,1)S(1)}, f32[2,1024]{1,0:T(2,128)S(1)}, f32[1024,128]{1,0:T(8,128)S(1)}, f32[1024,128]{1,0:T(8,128)S(1)}) custom-call(s32[32]{0:T(128)S(1)} %get-tuple-element.66.final_ref, s32[8]{0:T(128)S(1)} %get-tuple-element.190.count_ref, s32[1]{0:T(128)} %bitcast.first_ref, ...), custom_call_target="tpu_custom_call" | custom-call | flops 17179869184 | bytes 65536 | tf_op jit(solution)/shard_map/cond/branch_0_fun/attend/pallas_call | solution.py:270
  516.2 21.1 %collective-permute-done.46.rest_4_ = bf16[8,2,128,128]{3,2,1,0:T(8,128)(2,1)S(1)} collective-permute-done((bf16[8,2,128,128]{3,2,1,0:T(8,128)(2,1)S(1)}, bf16[8,2,128,128]{3,2,1,0:T(8,128)(2,1)S(1)}, u32[]{:S(2)}, u32[]{:S(2)}) %collective-permute-start.46) | collective-permute-done | bytes 524320 | tf_op jit(solution)/shard_map/cond/branch_0_fun/lines7_2/ppermute | solution.py:434
  537.3 13.5 %attend.30 = (bf16[1024,128]{1,0:T(8,128)(2,1)S(1)}, bf16[1024,128]{1,0:T(8,128)(2,1)S(1)}, f32[2,1024]{1,0:T(2,128)S(1)}, f32[1024,128]{1,0:T(8,128)S(1)}, f32[1024,128]{1,0:T(8,128)S(1)}) custom-call(s32[32]{0:T(128)S(1)} %get-tuple-element.66.final_ref, s32[8]{0:T(128)S(1)} %get-tuple-element.190.count_ref, s32[1]{0:T(128)} %bitcast.first_ref, ...), custom_call_target="tpu_custom_call" | custom-call | flops 17179869184 | bytes 65536 | tf_op jit(solution)/shard_map/cond/branch_0_fun/attend/pallas_call | solution.py:270
  554.9 13.5 %attend.31 = (bf16[1024,128]{1,0:T(8,128)(2,1)S(1)}, bf16[1024,128]{1,0:T(8,128)(2,1)S(1)}, f32[2,1024]{1,0:T(2,128)S(1)}, f32[1024,128]{1,0:T(8,128)S(1)}, f32[1024,128]{1,0:T(8,128)S(1)}) custom-call(s32[32]{0:T(128)S(1)} %get-tuple-element.66.final_ref, s32[8]{0:T(128)S(1)} %get-tuple-element.190.count_ref, s32[1]{0:T(128)} %bitcast.first_ref, ...), custom_call_target="tpu_custom_call" | custom-call | flops 17179869184 | bytes 65536 | tf_op jit(solution)/shard_map/cond/branch_0_fun/attend/pallas_call | solution.py:270
  (302 shorter events, 265.3 us)
Async XLA Ops:
  21.2 45.9 %collective-permute-start.159 = (bf16[2,2,1024,128]{3,2,1,0:T(8,128)(2,1)}, bf16[2,2,1024,128]{3,2,1,0:T(8,128)(2,1)}, u32[]{:S(2)}, u32[]{:S(2)}) collective-permute-start(bf16[2,2,1024,128]{3,2,1,0:T(8,128)(2,1)} %fusion.1), channel_id=1, source_target_pairs={{0,4},{4,8},{8,12},{12,16},{16,20},{20,24},{24,28},{1,5},{5,9},{9,... | collective-permute-start | bytes 3145736 | tf_op jit(solution)/shard_map/prev_kv0/ppermute | solution.py:361
  24.0 45.6 %collective-permute-start.160 = (bf16[2,2,1024,128]{3,2,1,0:T(8,128)(2,1)S(1)}, bf16[2,2,1024,128]{3,2,1,0:T(8,128)(2,1)}, u32[]{:S(2)}, u32[]{:S(2)}) collective-permute-start(bf16[2,2,1024,128]{3,2,1,0:T(8,128)(2,1)S(1)} %fusion), channel_id=1, source_target_pairs={{4,0},{8,4},{12,8},{16,12},{20,16},{24,20},{28,24},{5,1},{9,5},{13... | collective-permute-start | bytes 3145736 | tf_op jit(solution)/shard_map/next_qg0/ppermute | solution.py:363
  106.2 46.1 %collective-permute-start.4 = (bf16[8,2,128,128]{3,2,1,0:T(8,128)(2,1)S(1)}, bf16[8,2,128,128]{3,2,1,0:T(8,128)(2,1)S(1)}, u32[]{:S(2)}, u32[]{:S(2)}) collective-permute-start(bf16[8,2,128,128]{3,2,1,0:T(8,128)(2,1)S(1)} %get-tuple-element.90), channel_id=1, source_target_pairs={{0,24},{4,28},{8,16},{12,20},{16,8},{20,12},{24,0},{28,4},{1,25},{... | collective-permute-start | bytes 1572872 | tf_op jit(solution)/shard_map/cond/branch_0_fun/lines0_2/ppermute | solution.py:434
  107.7 68.2 %collective-permute-start.5 = (bf16[2,1,1024,128]{3,2,1,0:T(8,128)(2,1)S(1)}, bf16[2,1,1024,128]{3,2,1,0:T(8,128)(2,1)S(1)}, u32[]{:S(2)}, u32[]{:S(2)}) collective-permute-start(bf16[2,1,1024,128]{3,2,1,0:T(8,128)(2,1)S(1)} %get-tuple-element.91), channel_id=1, source_target_pairs={{0,4},{4,8},{8,12},{12,16},{16,20},{20,24},{24,28},{1,5},{5,9},{9,... | collective-permute-start | bytes 1572872 | tf_op jit(solution)/shard_map/cond/branch_0_fun/prev_kv2/ppermute | solution.py:443
  188.3 43.2 %collective-permute-start.8 = (bf16[20,2,128,128]{3,2,1,0:T(8,128)(2,1)}, bf16[20,2,128,128]{3,2,1,0:T(8,128)(2,1)S(1)}, u32[]{:S(2)}, u32[]{:S(2)}) collective-permute-start(bf16[20,2,128,128]{3,2,1,0:T(8,128)(2,1)} %copy-done.78), channel_id=1, source_target_pairs={{0,4},{4,0},{8,12},{12,8},{16,20},{20,16},{24,28},{28,24},{1,5},{5... | collective-permute-start | bytes 3932168 | tf_op jit(solution)/shard_map/cond/branch_0_fun/side2/ppermute | solution.py:439
  189.0 47.3 %collective-permute-start.10 = (bf16[8,2,128,128]{3,2,1,0:T(8,128)(2,1)}, bf16[8,2,128,128]{3,2,1,0:T(8,128)(2,1)S(1)}, u32[]{:S(2)}, u32[]{:S(2)}) collective-permute-start(bf16[8,2,128,128]{3,2,1,0:T(8,128)(2,1)} %copy-done.110), channel_id=1, source_target_pairs={{0,16},{4,20},{8,24},{12,28},{16,0},{20,4},{24,8},{28,12},{1,17},{... | collective-permute-start | bytes 1572872 | tf_op jit(solution)/shard_map/cond/branch_0_fun/lines1_1/ppermute | solution.py:434
  189.0 48.9 %collective-permute-start.11 = (bf16[2,1,1024,128]{3,2,1,0:T(8,128)(2,1)}, bf16[2,1,1024,128]{3,2,1,0:T(8,128)(2,1)S(1)}, u32[]{:S(2)}, u32[]{:S(2)}) collective-permute-start(bf16[2,1,1024,128]{3,2,1,0:T(8,128)(2,1)} %get-tuple-element.105), channel_id=1, source_target_pairs={{0,4},{4,8},{8,12},{12,16},{16,20},{20,24},{24,28},{1,5},{5,9},{9,... | collective-permute-start | bytes 1572872 | tf_op jit(solution)/shard_map/cond/branch_0_fun/prev_kv3/ppermute | solution.py:443
  192.3 47.0 %collective-permute-start.12 = (bf16[2,1,1024,128]{3,2,1,0:T(8,128)(2,1)}, bf16[2,1,1024,128]{3,2,1,0:T(8,128)(2,1)S(1)}, u32[]{:S(2)}, u32[]{:S(2)}) collective-permute-start(bf16[2,1,1024,128]{3,2,1,0:T(8,128)(2,1)} %get-tuple-element.106), channel_id=1, source_target_pairs={{4,0},{8,4},{12,8},{16,12},{20,16},{24,20},{28,24},{5,1},{9,5},{13... | collective-permute-start | bytes 1572872 | tf_op jit(solution)/shard_map/cond/branch_0_fun/next_qg3/ppermute | solution.py:445
  195.8 43.4 %collective-permute-start.9 = (bf16[8,2,128,128]{3,2,1,0:T(8,128)(2,1)}, bf16[8,2,128,128]{3,2,1,0:T(8,128)(2,1)S(1)}, u32[]{:S(2)}, u32[]{:S(2)}) collective-permute-start(bf16[8,2,128,128]{3,2,1,0:T(8,128)(2,1)} %copy-done.103), channel_id=1, source_target_pairs={{0,8},{4,12},{8,0},{12,4},{16,24},{20,28},{24,16},{28,20},{1,9},{5... | collective-permute-start | bytes 1572872 | tf_op jit(solution)/shard_map/cond/branch_0_fun/lines1_0/ppermute | solution.py:434
  244.9 43.0 %collective-permute-start.14 = (bf16[20,2,128,128]{3,2,1,0:T(8,128)(2,1)S(1)}, bf16[20,2,128,128]{3,2,1,0:T(8,128)(2,1)S(1)}, u32[]{:S(2)}, u32[]{:S(2)}) collective-permute-start(bf16[20,2,128,128]{3,2,1,0:T(8,128)(2,1)S(1)} %copy-done.73), channel_id=1, source_target_pairs={{0,4},{4,0},{8,12},{12,8},{16,20},{20,16},{24,28},{28,24},{1,5},{5... | collective-permute-start | bytes 3932168 | tf_op jit(solution)/shard_map/cond/branch_0_fun/side3/ppermute | solution.py:439
  245.3 45.9 %collective-permute-start.15 = (bf16[8,2,128,128]{3,2,1,0:T(8,128)(2,1)S(1)}, bf16[8,2,128,128]{3,2,1,0:T(8,128)(2,1)S(1)}, u32[]{:S(2)}, u32[]{:S(2)}) collective-permute-start(bf16[8,2,128,128]{3,2,1,0:T(8,128)(2,1)S(1)} %get-tuple-element.116), channel_id=1, source_target_pairs={{0,8},{4,12},{8,0},{12,4},{16,24},{20,28},{24,16},{28,20},{1,9},{5... | collective-permute-start | bytes 1572872 | tf_op jit(solution)/shard_map/cond/branch_0_fun/lines2_0/ppermute | solution.py:434
  245.3 45.9 %collective-permute-start.16 = (bf16[8,2,128,128]{3,2,1,0:T(8,128)(2,1)S(1)}, bf16[8,2,128,128]{3,2,1,0:T(8,128)(2,1)S(1)}, u32[]{:S(2)}, u32[]{:S(2)}) collective-permute-start(bf16[8,2,128,128]{3,2,1,0:T(8,128)(2,1)S(1)} %get-tuple-element.117), channel_id=1, source_target_pairs={{0,16},{4,20},{8,24},{12,28},{16,0},{20,4},{24,8},{28,12},{1,17},{... | collective-permute-start | bytes 1572872 | tf_op jit(solution)/shard_map/cond/branch_0_fun/lines2_1/ppermute | solution.py:434
  247.8 44.4 %collective-permute-start.17 = (bf16[2,1,1024,128]{3,2,1,0:T(8,128)(2,1)S(1)}, bf16[2,1,1024,128]{3,2,1,0:T(8,128)(2,1)S(1)}, u32[]{:S(2)}, u32[]{:S(2)}) collective-permute-start(bf16[2,1,1024,128]{3,2,1,0:T(8,128)(2,1)S(1)} %copy-done.160), channel_id=1, source_target_pairs={{0,4},{4,8},{8,12},{12,16},{16,20},{20,24},{24,28},{1,5},{5,9},{9,... | collective-permute-start | bytes 1572872 | tf_op jit(solution)/shard_map/cond/branch_0_fun/prev_kv4/ppermute | solution.py:443
  298.6 43.5 %collective-permute-start.21 = (bf16[20,2,128,128]{3,2,1,0:T(8,128)(2,1)S(1)}, bf16[20,2,128,128]{3,2,1,0:T(8,128)(2,1)S(1)}, u32[]{:S(2)}, u32[]{:S(2)}) collective-permute-start(bf16[20,2,128,128]{3,2,1,0:T(8,128)(2,1)S(1)} %copy-done.67), channel_id=1, source_target_pairs={{0,4},{4,0},{8,12},{12,8},{16,20},{20,16},{24,28},{28,24},{1,5},{5... | collective-permute-start | bytes 3932168 | tf_op jit(solution)/shard_map/cond/branch_0_fun/side4/ppermute | solution.py:439
  301.6 43.8 %collective-permute-start.22 = (bf16[8,2,128,128]{3,2,1,0:T(8,128)(2,1)S(1)}, bf16[8,2,128,128]{3,2,1,0:T(8,128)(2,1)S(1)}, u32[]{:S(2)}, u32[]{:S(2)}) collective-permute-start(bf16[8,2,128,128]{3,2,1,0:T(8,128)(2,1)S(1)} %get-tuple-element.133), channel_id=1, source_target_pairs={{0,8},{4,12},{8,0},{12,4},{16,24},{20,28},{24,16},{28,20},{1,9},{5... | collective-permute-start | bytes 1572872 | tf_op jit(solution)/shard_map/cond/branch_0_fun/lines3_0/ppermute | solution.py:434
  301.6 43.8 %collective-permute-start.23 = (bf16[8,2,128,128]{3,2,1,0:T(8,128)(2,1)S(1)}, bf16[8,2,128,128]{3,2,1,0:T(8,128)(2,1)S(1)}, u32[]{:S(2)}, u32[]{:S(2)}) collective-permute-start(bf16[8,2,128,128]{3,2,1,0:T(8,128)(2,1)S(1)} %get-tuple-element.134), channel_id=1, source_target_pairs={{0,16},{4,20},{8,24},{12,28},{16,0},{20,4},{24,8},{28,12},{1,17},{... | collective-permute-start | bytes 1572872 | tf_op jit(solution)/shard_map/cond/branch_0_fun/lines3_1/ppermute | solution.py:434
  303.1 52.5 %collective-permute-start.24 = (bf16[2,1,1024,128]{3,2,1,0:T(8,128)(2,1)S(1)}, bf16[2,1,1024,128]{3,2,1,0:T(8,128)(2,1)S(1)}, u32[]{:S(2)}, u32[]{:S(2)}) collective-permute-start(bf16[2,1,1024,128]{3,2,1,0:T(8,128)(2,1)S(1)} %copy-done.154), channel_id=1, source_target_pairs={{0,4},{4,8},{8,12},{12,16},{16,20},{20,24},{24,28},{1,5},{5,9},{9,... | collective-permute-start | bytes 1572872 | tf_op jit(solution)/shard_map/cond/branch_0_fun/prev_kv5/ppermute | solution.py:443
  359.1 47.3 %collective-permute-start.29 = (bf16[8,2,128,128]{3,2,1,0:T(8,128)(2,1)S(1)}, bf16[8,2,128,128]{3,2,1,0:T(8,128)(2,1)S(1)}, u32[]{:S(2)}, u32[]{:S(2)}) collective-permute-start(bf16[8,2,128,128]{3,2,1,0:T(8,128)(2,1)S(1)} %get-tuple-element.150), channel_id=1, source_target_pairs={{0,8},{4,12},{8,0},{12,4},{16,24},{20,28},{24,16},{28,20},{1,9},{5... | collective-permute-start | bytes 1572872 | tf_op jit(solution)/shard_map/cond/branch_0_fun/lines4_0/ppermute | solution.py:434
  359.2 47.2 %collective-permute-start.30 = (bf16[8,2,128,128]{3,2,1,0:T(8,128)(2,1)S(1)}, bf16[8,2,128,128]{3,2,1,0:T(8,128)(2,1)S(1)}, u32[]{:S(2)}, u32[]{:S(2)}) collective-permute-start(bf16[8,2,128,128]{3,2,1,0:T(8,128)(2,1)S(1)} %get-tuple-element.151), channel_id=1, source_target_pairs={{0,16},{4,20},{8,24},{12,28},{16,0},{20,4},{24,8},{28,12},{1,17},{... | collective-permute-start | bytes 1572872 | tf_op jit(solution)/shard_map/cond/branch_0_fun/lines4_1/ppermute | solution.py:434
  362.5 49.9 %collective-permute-start.31 = (bf16[2,1,1024,128]{3,2,1,0:T(8,128)(2,1)}, bf16[2,1,1024,128]{3,2,1,0:T(8,128)(2,1)S(1)}, u32[]{:S(2)}, u32[]{:S(2)}) collective-permute-start(bf16[2,1,1024,128]{3,2,1,0:T(8,128)(2,1)} %get-tuple-element.152), channel_id=1, source_target_pairs={{0,4},{4,8},{8,12},{12,16},{16,20},{20,24},{24,28},{1,5},{5,9},{9,... | collective-permute-start | bytes 1572872 | tf_op jit(solution)/shard_map/cond/branch_0_fun/prev_kv6/ppermute | solution.py:443
  417.2 43.0 %collective-permute-start.35 = (bf16[20,2,128,128]{3,2,1,0:T(8,128)(2,1)S(1)}, bf16[20,2,128,128]{3,2,1,0:T(8,128)(2,1)S(1)}, u32[]{:S(2)}, u32[]{:S(2)}) collective-permute-start(bf16[20,2,128,128]{3,2,1,0:T(8,128)(2,1)S(1)} %copy-done.55), channel_id=1, source_target_pairs={{0,4},{4,0},{8,12},{12,8},{16,20},{20,16},{24,28},{28,24},{1,5},{5... | collective-permute-start | bytes 3932168 | tf_op jit(solution)/shard_map/cond/branch_0_fun/side6/ppermute | solution.py:439
  417.7 45.9 %collective-permute-start.36 = (bf16[8,2,128,128]{3,2,1,0:T(8,128)(2,1)S(1)}, bf16[8,2,128,128]{3,2,1,0:T(8,128)(2,1)S(1)}, u32[]{:S(2)}, u32[]{:S(2)}) collective-permute-start(bf16[8,2,128,128]{3,2,1,0:T(8,128)(2,1)S(1)} %get-tuple-element.167), channel_id=1, source_target_pairs={{0,8},{4,12},{8,0},{12,4},{16,24},{20,28},{24,16},{28,20},{1,9},{5... | collective-permute-start | bytes 1572872 | tf_op jit(solution)/shard_map/cond/branch_0_fun/lines5_0/ppermute | solution.py:434
  417.7 45.9 %collective-permute-start.37 = (bf16[8,2,128,128]{3,2,1,0:T(8,128)(2,1)S(1)}, bf16[8,2,128,128]{3,2,1,0:T(8,128)(2,1)S(1)}, u32[]{:S(2)}, u32[]{:S(2)}) collective-permute-start(bf16[8,2,128,128]{3,2,1,0:T(8,128)(2,1)S(1)} %get-tuple-element.168), channel_id=1, source_target_pairs={{0,16},{4,20},{8,24},{12,28},{16,0},{20,4},{24,8},{28,12},{1,17},{... | collective-permute-start | bytes 1572872 | tf_op jit(solution)/shard_map/cond/branch_0_fun/lines5_1/ppermute | solution.py:434
  419.6 47.9 %collective-permute-start.38 = (bf16[2,1,1024,128]{3,2,1,0:T(8,128)(2,1)S(1)}, bf16[2,1,1024,128]{3,2,1,0:T(8,128)(2,1)S(1)}, u32[]{:S(2)}, u32[]{:S(2)}) collective-permute-start(bf16[2,1,1024,128]{3,2,1,0:T(8,128)(2,1)S(1)} %copy-done.144), channel_id=1, source_target_pairs={{0,4},{4,8},{8,12},{12,16},{16,20},{20,24},{24,28},{1,5},{5,9},{9,... | collective-permute-start | bytes 1572872 | tf_op jit(solution)/shard_map/cond/branch_0_fun/prev_kv7/ppermute | solution.py:443
  (97 other events, 1745.3 us)
